TPU v7x, 32 devices: a whole 2x2x4 slice. The times are simulated.
32 devices in a mesh: dp: 16 (over z, y, core), tensor: 2 (over x).
Axes of the slice: x: 2, y: 2, z: 4, core: 2. Of those that a mesh axis runs over, the one named last changes fastest.
Arguments:
- tokens: bfloat16 [16384, 1536], P(('dp', 'tensor')), may hold values from -6 to 6
- attn_gain: bfloat16 [1536], P('dp'), may hold values from 0.099609375 to 1.8984375
- ffn_gain: bfloat16 [1536], P('dp'), may hold values from 0.099609375 to 1.8984375
- router: bfloat16 [1536, 8], P('dp'), may hold values from -0.078125 to 0.078125
- w_query: bfloat16 [1536, 1536], P('dp', 'tensor'), may hold values from -0.15625 to 0.15625
- key_matrix: bfloat16 [1536, 256], P('dp', 'tensor'), may hold values from -0.15625 to 0.15625
- value_matrix: bfloat16 [1536, 256], P('dp', 'tensor'), may hold values from -0.15625 to 0.15625
- w_out_t: bfloat16 [1536, 1536], P('dp', 'tensor'), may hold values from -1.75 to 1.75
- w_gate: bfloat16 [8, 1536, 768], P(None, 'dp', 'tensor'), may hold values from -0.15625 to 0.15625
- w_up: bfloat16 [8, 1536, 768], P(None, 'dp', 'tensor'), may hold values from -0.15625 to 0.15625
- w_down_t: bfloat16 [8, 1536, 768], P(None, 'dp', 'tensor'), may hold values from -0.21875 to 0.21875
- lengths: int32 [16], P('dp'), may hold values from 513 to 1024, as said below
- routes: int32 [16384, 4], P('dp'), may hold values from 0 to 7, all different within a row
- priority: int32 [16384, 4], P('dp'), may hold values from 0 to 4095, as said below
- cotangent: bfloat16 [16384, 1536], P(('dp', 'tensor')), may hold values from -6 to 6
Outputs:
- block_out: bfloat16 [16384, 1536], P(('dp', 'tensor'))
- input_grad: float32 [16384, 1536], P(('dp', 'tensor'))
- attn_gain_grad: float32 [1536], P('dp')
- ffn_gain_grad: float32 [1536], P('dp')
- router_grad: float32 [1536, 8], P('dp')
- w_query_grad: float32 [1536, 1536], P('dp', 'tensor')
- w_key_grad: float32 [1536, 256], P('dp', 'tensor')
- w_value_grad: float32 [1536, 256], P('dp', 'tensor')
- w_out_t_grad: float32 [1536, 1536], P('dp', 'tensor')
- w_gate_grad: float32 [8, 1536, 768], P(None, 'dp', 'tensor')
- w_up_grad: float32 [8, 1536, 768], P(None, 'dp', 'tensor')
- w_down_t_grad: float32 [8, 1536, 768], P(None, 'dp', 'tensor')
Inputs may be any that keep to these rules, and one draw needn't show every extreme that they name: `lengths`: every length is over half of 1024; some sequence has exactly 1024. `priority`: within each group of 1024 rows the entries are a permutation of 0 to 4095.
All inputs are finite; a program needn't handle non-finite values.
Results may differ from a plain program's by a relative error of at most 0.022.
Values may be sent and summed in bfloat16 or wider, within the bound.
A program may use at most 320 MiB of HBM per device.

v0:
```python
import jax
import jax.numpy as jnp
from jax import lax
from jax.sharding import PartitionSpec as P

MODEL_WIDTH = 1536
QUERY_HEADS = 12
KEY_VALUE_HEADS = 2
HEAD_SIZE = 128
TOP = 4
EXPERTS = 8
SLOT_POSITIONS = 1024
SEQS = 1
GROUP = 1024
CAP = 512


EPSILON = 1e-06
ROPE_BASE = 10000.0
MASKED = -1e30
FLOAT = jnp.float32
BFLOAT = jnp.bfloat16


def route_slots(routes, priority, valid_rows, capacity):
    local_tokens = routes.shape[0]
    top_k = routes.shape[1]
    pair_count = local_tokens * top_k
    experts_flat = routes.reshape(pair_count)
    ranks_flat = priority.reshape(pair_count)
    live_pairs = jnp.repeat(valid_rows.astype(jnp.int32), top_k)
    pair_ids = jnp.arange(pair_count, dtype=jnp.int32)
    ordering = jnp.zeros((pair_count,), jnp.int32).at[ranks_flat].set(pair_ids)
    columns = jnp.arange(EXPERTS, dtype=jnp.int32)
    onehot = (experts_flat[ordering][:, None] == columns[None, :]).astype(jnp.int32) * live_pairs[
        ordering
    ][:, None]
    earlier = jnp.cumsum(onehot, axis=0, dtype=jnp.int32) - onehot
    rank_sorted = jnp.sum(earlier * onehot, axis=1, dtype=jnp.int32)
    place_rank = rank_sorted[ranks_flat]
    keeping = (live_pairs > 0) & (place_rank < capacity)
    slot_ids = jnp.where(keeping, experts_flat * capacity + place_rank, EXPERTS * capacity)
    slot_table = (
        jnp.full((EXPERTS * capacity + 1,), pair_count, jnp.int32).at[slot_ids].set(pair_ids)
    )
    return (
        keeping.reshape(local_tokens, top_k),
        slot_ids.reshape(local_tokens, top_k),
        slot_table[: EXPERTS * capacity],
    )


def rope_tables(places):
    half_dim = HEAD_SIZE // 2
    frequency = ROPE_BASE ** (-jnp.arange(half_dim, dtype=FLOAT) / half_dim)
    angles = places.astype(FLOAT)[:, None] * frequency[None, :]
    return (jnp.cos(angles)[:, None, :], jnp.sin(angles)[:, None, :])


def apply_rotary(values, cosine_lookup, sine_lookup):
    half_dim = values.shape[-1] // 2
    first_half = values[..., :half_dim]
    second_half = values[..., half_dim:]
    return jnp.concatenate(
        [
            first_half * cosine_lookup - second_half * sine_lookup,
            second_half * cosine_lookup + first_half * sine_lookup,
        ],
        axis=-1,
    )


def rotate_back(gradients, cosine_lookup, sine_lookup):
    half_dim = gradients.shape[-1] // 2
    first_half = gradients[..., :half_dim]
    second_half = gradients[..., half_dim:]
    return jnp.concatenate(
        [
            first_half * cosine_lookup + second_half * sine_lookup,
            second_half * cosine_lookup - first_half * sine_lookup,
        ],
        axis=-1,
    )


def norm_forward(values, gain_vec):
    scale_rows = lax.rsqrt(jnp.mean(values * values, axis=1, keepdims=True) + EPSILON)
    return ((values * scale_rows * gain_vec).astype(BFLOAT), scale_rows)


def norm_backward(values, scale_rows, gain_vec, incoming):
    gain_term = jnp.sum(incoming * values * scale_rows, axis=0)
    inner_sum = jnp.mean(incoming * gain_vec * values, axis=1, keepdims=True)
    return (scale_rows * gain_vec * incoming - values * scale_rows**3 * inner_sum, gain_term)


def matmul_t(left, right):
    return lax.dot_general(left, right, (((1,), (1,)), ((), ())), preferred_element_type=FLOAT)


def matmul_tn(left, right):
    return lax.dot_general(left, right, (((0,), (0,)), ((), ())), preferred_element_type=FLOAT)


def gather_layer(attn_gain, ffn_gain, router, w_query, key_matrix, value_matrix, w_out_t):
    return (
        lax.all_gather(attn_gain, "dp", axis=0, tiled=True),
        lax.all_gather(ffn_gain, "dp", axis=0, tiled=True),
        lax.all_gather(router, "dp", axis=0, tiled=True),
        lax.all_gather(w_query, "dp", axis=0, tiled=True),
        lax.all_gather(key_matrix, "dp", axis=0, tiled=True),
        lax.all_gather(value_matrix, "dp", axis=0, tiled=True),
        lax.all_gather(w_out_t, "dp", axis=0, tiled=True),
    )


def gather_experts(w_gate, w_up, w_down_t):
    return (
        lax.all_gather(w_gate, "dp", axis=1, tiled=True),
        lax.all_gather(w_up, "dp", axis=1, tiled=True),
        lax.all_gather(w_down_t, "dp", axis=1, tiled=True),
    )


def masked_scores(query_block, key_part, places, first_row, block_rows, valid_part):
    key_count = key_part.shape[0]
    scores = jnp.einsum(
        "qgrd,kgd->grqk", query_block, key_part, preferred_element_type=FLOAT
    ) * HEAD_SIZE ** (-0.5)
    allowed = (
        places[None, :key_count] <= places[first_row : first_row + block_rows, None]
    ) & valid_part[None, :]
    return jnp.where(allowed, scores, MASKED)


def attend(query_rows, every_key, every_value, valid_keys):
    length = query_rows.shape[0]
    block_rows = min(512, length)
    places = jnp.arange(length, dtype=jnp.int32)
    outputs = []
    totals = []
    for first_row in range(0, length, block_rows):
        last_key = first_row + block_rows
        query_block = query_rows[first_row:last_key]
        scores = masked_scores(
            query_block, every_key[:last_key], places, first_row, block_rows, valid_keys[:last_key]
        )
        row_peak = jnp.max(scores, axis=-1, keepdims=True)
        weights = jnp.exp(scores - row_peak)
        norm_sum = jnp.sum(weights, axis=-1, keepdims=True)
        prob_low = (weights / norm_sum).astype(BFLOAT)
        outputs.append(
            jnp.einsum(
                "grqk,kgd->qgrd", prob_low, every_value[:last_key], preferred_element_type=FLOAT
            )
        )
        totals.append((row_peak + jnp.log(norm_sum))[..., 0])
    return (jnp.concatenate(outputs, axis=0), jnp.concatenate(totals, axis=-1))


def attend_back(query_rows, every_key, every_value, valid_keys, log_totals, grad_heads):
    length = query_rows.shape[0]
    block_rows = min(512, length)
    places = jnp.arange(length, dtype=jnp.int32)
    scale_value = HEAD_SIZE ** (-0.5)
    key_grad = jnp.zeros(every_key.shape, FLOAT)
    value_grad = jnp.zeros(every_value.shape, FLOAT)
    query_grads = []
    for first_row in range(0, length, block_rows):
        last_key = first_row + block_rows
        query_block = query_rows[first_row:last_key]
        grad_block = grad_heads[first_row:last_key]
        key_part = every_key[:last_key]
        scores = masked_scores(
            query_block, key_part, places, first_row, block_rows, valid_keys[:last_key]
        )
        probabilities = jnp.exp(scores - log_totals[..., first_row:last_key, None])
        prob_low = probabilities.astype(BFLOAT)
        dprobs = jnp.einsum(
            "qgrd,kgd->grqk", grad_block, every_value[:last_key], preferred_element_type=FLOAT
        )
        inner_sum = jnp.sum(probabilities * dprobs, axis=-1, keepdims=True)
        dscores = (probabilities * (dprobs - inner_sum)).astype(BFLOAT)
        query_grads.append(
            jnp.einsum("grqk,kgd->qgrd", dscores, key_part, preferred_element_type=FLOAT)
            * scale_value
        )
        key_grad = key_grad.at[:last_key].add(
            jnp.einsum("grqk,qgrd->kgd", dscores, query_block, preferred_element_type=FLOAT)
            * scale_value
        )
        value_grad = value_grad.at[:last_key].add(
            jnp.einsum("grqk,qgrd->kgd", prob_low, grad_block, preferred_element_type=FLOAT)
        )
    return (jnp.concatenate(query_grads, axis=0), key_grad, value_grad)


def shards(
    tokens,
    attn_gain,
    ffn_gain,
    router,
    w_query,
    key_matrix,
    value_matrix,
    w_out_t,
    w_gate,
    w_up,
    w_down_t,
    lengths,
    routes,
    priority,
    cotangent,
):
    tensor_split_count = lax.axis_size("tensor")
    my_index = lax.axis_index("tensor")
    local_rows = tokens.shape[0]
    head_group_count = KEY_VALUE_HEADS // tensor_split_count
    heads_per_group = QUERY_HEADS // KEY_VALUE_HEADS
    gain_one, gain_two, router_full, query_full, key_full, value_full, out_full = gather_layer(
        attn_gain, ffn_gain, router, w_query, key_matrix, value_matrix, w_out_t
    )
    gate_full, up_full, down_full = gather_experts(w_gate, w_up, w_down_t)
    places = jnp.arange(GROUP, dtype=jnp.int32) % SLOT_POSITIONS
    seq_of = jnp.arange(GROUP, dtype=jnp.int32) // SLOT_POSITIONS
    valid_rows = places < lengths[seq_of]
    valid_mine = lax.dynamic_slice_in_dim(valid_rows, my_index * local_rows, local_rows).astype(
        FLOAT
    )[:, None]
    cosine_lookup, sine_lookup = rope_tables(places)
    inputs = tokens.astype(FLOAT)
    normed_mine, scale_one = norm_forward(inputs, gain_one.astype(FLOAT))
    normed_input = lax.all_gather(normed_mine, "tensor", axis=0, tiled=True)
    query_rot = apply_rotary(
        jnp.dot(normed_input, query_full, preferred_element_type=FLOAT).reshape(
            GROUP, head_group_count * heads_per_group, HEAD_SIZE
        ),
        cosine_lookup,
        sine_lookup,
    ).astype(BFLOAT)
    key_rot = apply_rotary(
        jnp.dot(normed_input, key_full, preferred_element_type=FLOAT).reshape(
            GROUP, head_group_count, HEAD_SIZE
        ),
        cosine_lookup,
        sine_lookup,
    ).astype(BFLOAT)
    value_low = jnp.dot(normed_input, value_full, preferred_element_type=FLOAT).astype(BFLOAT)
    query_seq = query_rot.reshape(
        SEQS, SLOT_POSITIONS, head_group_count, heads_per_group, HEAD_SIZE
    )
    key_seq = key_rot.reshape(SEQS, SLOT_POSITIONS, head_group_count, HEAD_SIZE)
    value_seq = value_low.reshape(SEQS, SLOT_POSITIONS, head_group_count, HEAD_SIZE)
    valid_seq = valid_rows.reshape(SEQS, SLOT_POSITIONS)
    heads_seq, log_totals = lax.map(
        lambda one_item: attend(*one_item), (query_seq, key_seq, value_seq, valid_seq)
    )
    heads_low = heads_seq.reshape(GROUP, head_group_count * heads_per_group * HEAD_SIZE).astype(
        BFLOAT
    )
    attn_terms = matmul_t(heads_low, out_full)
    branch = lax.psum_scatter(
        attn_terms.astype(jnp.bfloat16), "tensor", scatter_dimension=0, tiled=True
    ).astype(jnp.float32)
    middle = inputs + branch
    normed_two_mine, scale_two = norm_forward(middle, gain_two.astype(FLOAT))
    normed_two = lax.all_gather(normed_two_mine, "tensor", axis=0, tiled=True)
    logits = jnp.dot(normed_two, router_full, preferred_element_type=FLOAT)
    chosen = jnp.take_along_axis(logits, routes, axis=1)
    soft_gates = jax.nn.softmax(chosen, axis=1)
    keeping, slot_ids, slot_table = route_slots(routes, priority, valid_rows, CAP)
    keep_f = keeping.astype(FLOAT)
    gates = soft_gates * keep_f
    filled = slot_table < GROUP * TOP
    token_rows = jnp.minimum(slot_table // TOP, GROUP - 1)
    expert_in = jnp.where(filled[:, None], normed_two[token_rows], jnp.zeros((), BFLOAT)).reshape(
        EXPERTS, CAP, MODEL_WIDTH
    )
    gate_pre = jnp.einsum("ecd,edf->ecf", expert_in, gate_full, preferred_element_type=FLOAT)
    up_pre = jnp.einsum("ecd,edf->ecf", expert_in, up_full, preferred_element_type=FLOAT)
    sigmoid_a = jax.nn.sigmoid(gate_pre)
    active = gate_pre * sigmoid_a
    hidden = (active * up_pre).astype(BFLOAT)
    expert_out = jnp.einsum(
        "ecf,edf->ecd", hidden, down_full, preferred_element_type=FLOAT
    ).reshape(EXPERTS * CAP, MODEL_WIDTH)
    slot_rows = jnp.minimum(slot_ids, EXPERTS * CAP - 1)
    picked = expert_out[slot_rows]
    ffn_terms = jnp.sum(gates[:, :, None] * picked, axis=1)
    ffn_sum = lax.psum_scatter(
        ffn_terms.astype(jnp.bfloat16), "tensor", scatter_dimension=0, tiled=True
    ).astype(jnp.float32)
    block_out = (valid_mine * (middle + ffn_sum)).astype(BFLOAT)
    grad_out = cotangent.astype(FLOAT) * valid_mine
    grad_low = grad_out.astype(BFLOAT)
    grad_ffn = lax.all_gather(grad_low, "tensor", axis=0, tiled=True)
    pair_rows = jnp.minimum(slot_table, GROUP * TOP - 1)
    slot_gate = jnp.where(filled, gates.reshape(GROUP * TOP)[pair_rows], 0.0)
    grad_expert = (
        (slot_gate[:, None] * grad_ffn[token_rows].astype(FLOAT))
        .astype(BFLOAT)
        .reshape(EXPERTS, CAP, MODEL_WIDTH)
    )
    gate_grad_terms = jnp.einsum(
        "td,tkd->tk", grad_ffn.astype(FLOAT), picked, precision=lax.Precision.HIGHEST
    )
    gate_grads = lax.psum(gate_grad_terms, "tensor")
    soft_grad = gate_grads * keep_f
    dchosen = soft_gates * (soft_grad - jnp.sum(soft_gates * soft_grad, axis=1, keepdims=True))
    expert_ids = jnp.arange(EXPERTS, dtype=jnp.int32)
    dlogits = jnp.sum(
        (routes[:, :, None] == expert_ids[None, None, :]).astype(FLOAT) * dchosen[:, :, None],
        axis=1,
    ).astype(BFLOAT)
    router_grad = matmul_tn(normed_two, dlogits)
    hidden_grad = jnp.einsum("ecd,edf->ecf", grad_expert, down_full, preferred_element_type=FLOAT)
    gate_low = (hidden_grad * up_pre * sigmoid_a * (1.0 + gate_pre * (1.0 - sigmoid_a))).astype(
        BFLOAT
    )
    up_low = (hidden_grad * active).astype(BFLOAT)
    expert_in_grad = (
        jnp.einsum("ecf,edf->ecd", gate_low, gate_full, preferred_element_type=FLOAT)
        + jnp.einsum("ecf,edf->ecd", up_low, up_full, preferred_element_type=FLOAT)
    ).reshape(EXPERTS * CAP, MODEL_WIDTH)
    gate_w_grad = jnp.einsum("ecd,ecf->edf", expert_in, gate_low, preferred_element_type=FLOAT)
    up_w_grad = jnp.einsum("ecd,ecf->edf", expert_in, up_low, preferred_element_type=FLOAT)
    down_w_grad = jnp.einsum("ecd,ecf->edf", grad_expert, hidden, preferred_element_type=FLOAT)
    normed_two_terms = jnp.sum(keep_f[:, :, None] * expert_in_grad[slot_rows], axis=1)
    normed_two_grad = lax.psum_scatter(
        normed_two_terms.astype(jnp.bfloat16), "tensor", scatter_dimension=0, tiled=True
    ).astype(jnp.float32)
    normed_two_grad = normed_two_grad + matmul_t(
        lax.dynamic_slice_in_dim(dlogits, my_index * local_rows, local_rows), router_full
    )
    middle_part, gain_two_grad = norm_backward(
        middle, scale_two, gain_two.astype(FLOAT), normed_two_grad
    )
    middle_grad = grad_out + middle_part
    grad_branch = lax.all_gather(middle_grad.astype(BFLOAT), "tensor", axis=0, tiled=True)
    heads_grad = jnp.dot(grad_branch, out_full, preferred_element_type=FLOAT).astype(BFLOAT)
    out_grad = matmul_tn(grad_branch, heads_low)
    heads_grad_seq = heads_grad.reshape(
        SEQS, SLOT_POSITIONS, head_group_count, heads_per_group, HEAD_SIZE
    )
    query_back, key_back, value_back = lax.map(
        lambda one_item: attend_back(*one_item),
        (query_seq, key_seq, value_seq, valid_seq, log_totals, heads_grad_seq),
    )
    query_raw_grad = (
        rotate_back(
            query_back.reshape(GROUP, head_group_count * heads_per_group, HEAD_SIZE),
            cosine_lookup,
            sine_lookup,
        )
        .reshape(GROUP, head_group_count * heads_per_group * HEAD_SIZE)
        .astype(BFLOAT)
    )
    key_raw_grad = (
        rotate_back(
            key_back.reshape(GROUP, head_group_count, HEAD_SIZE), cosine_lookup, sine_lookup
        )
        .reshape(GROUP, head_group_count * HEAD_SIZE)
        .astype(BFLOAT)
    )
    value_raw_grad = value_back.reshape(GROUP, head_group_count * HEAD_SIZE).astype(BFLOAT)
    normed_terms = (
        matmul_t(query_raw_grad, query_full)
        + matmul_t(key_raw_grad, key_full)
        + matmul_t(value_raw_grad, value_full)
    )
    query_w_grad = matmul_tn(normed_input, query_raw_grad)
    key_w_grad = matmul_tn(normed_input, key_raw_grad)
    value_w_grad = matmul_tn(normed_input, value_raw_grad)
    normed_grad = lax.psum_scatter(
        normed_terms.astype(jnp.bfloat16), "tensor", scatter_dimension=0, tiled=True
    ).astype(jnp.float32)
    input_part, gain_one_grad = norm_backward(
        inputs, scale_one, gain_one.astype(FLOAT), normed_grad
    )
    input_grad = middle_grad + input_part
    layer_grads = (
        lax.psum_scatter(gain_one_grad, "dp", scatter_dimension=0, tiled=True),
        lax.psum_scatter(gain_two_grad, "dp", scatter_dimension=0, tiled=True),
        lax.psum_scatter(router_grad, "dp", scatter_dimension=0, tiled=True),
        lax.psum_scatter(query_w_grad, "dp", scatter_dimension=0, tiled=True),
        lax.psum_scatter(key_w_grad, "dp", scatter_dimension=0, tiled=True),
        lax.psum_scatter(value_w_grad, "dp", scatter_dimension=0, tiled=True),
        lax.psum_scatter(out_grad, "dp", scatter_dimension=0, tiled=True),
    )
    expert_grads = (
        lax.psum_scatter(gate_w_grad, "dp", scatter_dimension=1, tiled=True),
        lax.psum_scatter(up_w_grad, "dp", scatter_dimension=1, tiled=True),
        lax.psum_scatter(down_w_grad, "dp", scatter_dimension=1, tiled=True),
    )
    gain_one_sum, gain_two_sum = lax.psum((layer_grads[0], layer_grads[1]), "tensor")
    return (
        block_out,
        input_grad,
        gain_one_sum,
        gain_two_sum,
        layer_grads[2],
        layer_grads[3],
        layer_grads[4],
        layer_grads[5],
        layer_grads[6],
        expert_grads[0],
        expert_grads[1],
        expert_grads[2],
    )


def solution(mesh):
    return jax.shard_map(
        shards,
        mesh=mesh,
        in_specs=(
            P(("dp", "tensor"), None),
            P("dp"),
            P("dp"),
            P("dp", None),
            P("dp", "tensor"),
            P("dp", "tensor"),
            P("dp", "tensor"),
            P("dp", "tensor"),
            P(None, "dp", "tensor"),
            P(None, "dp", "tensor"),
            P(None, "dp", "tensor"),
            P("dp"),
            P("dp", None),
            P("dp", None),
            P(("dp", "tensor"), None),
        ),
        out_specs=(
            P(("dp", "tensor"), None),
            P(("dp", "tensor"), None),
            P("dp"),
            P("dp"),
            P("dp", None),
            P("dp", "tensor"),
            P("dp", "tensor"),
            P("dp", "tensor"),
            P("dp", "tensor"),
            P(None, "dp", "tensor"),
            P(None, "dp", "tensor"),
            P(None, "dp", "tensor"),
        ),
        check_vma=False,
    )
```

profile of v0, /device:TPU:0, one launch (start us, length us, event | category | flops | bytes accessed | tf_op | source)
XLA Modules:
  0.0 2075.4 jit_solution(1864313645023574924)
XLA Ops:
  10.9 36.0 %all-reduce.8 = (bf16[1536]{0:T(1024)(128)(2,1)S(1)}, bf16[1536]{0:T(1024)(128)(2,1)}) all-reduce(bf16[1536]{0:T(1024)(128)(2,1)S(1)} %dynamic-update-slice.12, bf16[1536]{0:T(1024)(128)(2,1)S(1)} %dynamic-update-slice.13), channel_id=1, replica_groups=mesh['dp'=16,'tensor'=2] {'dp'}, use_global_device_ids=true, to_apply=%add.2 | all-reduce | flops 3072 | bytes 12288
  49.9 3.0 fusion.38
  54.5 18.2 all_gather.45
  73.5 21.8 %all_gather.44 = bf16[1536,128]{1,0:T(8,128)(2,1)} all-gather(bf16[96,128]{1,0:T(8,128)(2,1)S(1)} %copy-done.83), channel_id=1, replica_groups=mesh['dp'=16,'tensor'=2] {'dp'}, dimensions={0}, use_global_device_ids=true | all-gather | bytes 417792 | tf_op jit(solution)/shard_map/all_gather | solution.py:112
  96.5 3.0 multiply_cosine_fusion
  100.5 3.2 convolution_bitcast_fusion.1
  107.5 32.3 %all-gather.13.cloned.1.call-done = bf16[1536,768]{1,0:T(8,128)(2,1)} async-done(((bf16[96,768]{1,0:T(8,128)(2,1)}), bf16[1536,768]{1,0:T(8,128)(2,1)}) %all-gather.13.cloned.1.call-update) | async-done | bytes 2359312 | tf_op jit(solution)/shard_map/all_gather | solution.py:110
  139.8 4.4 fusion.149
  148.2 3.7 copy.233
  152.0 3.0 subtract_convert_fusion.1
  169.8 13.4 all-gather.15.cloned.1.call-done
  183.1 5.7 convolution_convert_fusion
  191.8 39.3 %reduce-scatter.15.cloned.1.call-done = bf16[512,1536]{1,0:T(8,128)(2,1)} async-done(((bf16[1024,1536]{1,0:T(8,128)(2,1)}), bf16[512,1536]{1,0:T(8,128)(2,1)}) %reduce-scatter.15.cloned.1.call-update) | async-done | bytes 1572880 | tf_op jit(solution)/shard_map/reduce_scatter | solution.py:262
  240.1 15.5 scatter_custom_fusion
  255.7 23.0 %gather_fusion.1 = s32[4096]{0:T(1024)S(1)} fusion(s32[4096]{0:T(1024)S(1)} %reshape.782, s32[4096]{0:T(1024)S(1)} %fusion.110), kind=kCustom, calls=%fused_computation.1 | custom fusion | bytes 49152 | tf_op jit(solution)/shard_map/gather | solution.py:35
  278.7 23.0 %gather_fusion = s32[4096]{0:T(1024)S(1)} fusion(s32[4096]{0:T(1024)S(1)} %reshape.780, s32[4096]{0:T(1024)S(1)} %fusion.110), kind=kCustom, calls=%fused_computation | custom fusion | bytes 49152 | tf_op jit(solution)/shard_map/gather | solution.py:35
  304.9 23.0 %gather_fusion.2 = s32[4096]{0:T(1024)S(1)} fusion(s32[4096]{0:T(1024)S(1)} %fusion.102, s32[4096]{0:T(1024)S(1)} %broadcast_clamp_fusion.1), kind=kCustom, calls=%fused_computation.2 | custom fusion | bytes 49152 | tf_op jit(solution)/shard_map/gather | solution.py:40
  329.9 15.5 scatter_custom_fusion.1
  346.6 21.7 %all-gather = bf16[16,96,8]{1,2,0:T(8,128)(2,1)S(1)} all-gather(bf16[1,96,8]{1,2,0:T(8,128)(2,1)S(1)} %bitcast.288), channel_id=1, replica_groups=mesh['dp'=16,'tensor'=2] {'dp'}, dimensions={0}, use_global_device_ids=true | all-gather | bytes 26112 | tf_op jit(solution)/shard_map/all_gather | solution.py:109
  371.3 27.8 %gather_fusion.6 = bf16[4096,1536]{1,0:T(8,128)(2,1)} fusion(bf16[1024,1536]{1,0:T(8,128)(2,1)} %all-gather.25.cloned.1.call-done, s32[4096]{0:T(1024)S(1)} %get-tuple-element.183), kind=kCustom, calls=%fused_computation.6 | custom fusion | bytes 25182208 | tf_op jit(solution)/shard_map/gather | solution.py:300
  399.1 17.7 copy.188
  416.8 27.8 %gather_fusion.3 = bf16[4096,1536]{1,0:T(8,128)(2,1)} fusion(bf16[1024,1536]{1,0:T(8,128)(2,1)} %all-gather.17.cloned.1.call-done, s32[4096]{0:T(1024)S(1)} %get-tuple-element.183), kind=kCustom, calls=%fused_computation.3 | custom fusion | bytes 25182208 | tf_op jit(solution)/shard_map/gather | solution.py:276
  444.5 17.7 copy.181
  463.2 24.5 %gather_fusion.8 = f32[4096]{0:T(1024)S(1)} fusion(f32[1024,8]{0,1:T(8,128)S(1)} %fusion.150, s32[4096]{0:T(1024)S(1)} %reshape.860), kind=kCustom, calls=%fused_computation.8 | custom fusion | bytes 65536 | tf_op jit(solution)/shard_map/jit(take_along_axis)/gather | solution.py:269
  488.5 14.2 fusion.8
  502.7 15.4 multiply_convert_fusion.3
  518.1 55.0 %all-gather.23.cloned.1.call-done = bf16[8,1536,384]{2,1,0:T(8,128)(2,1)} async-done(((bf16[8,96,384]{2,1,0:T(8,128)(2,1)}), bf16[8,1536,384]{2,1,0:T(8,128)(2,1)}) %all-gather.23.cloned.1.call-update) | async-done | bytes 9437200 | tf_op jit(solution)/shard_map/all_gather | solution.py:121
  573.2 15.8 fusion.151
  589.0 35.3 %gather_fusion.4 = f32[4096,1536]{1,0:T(8,128)} fusion(f32[4096,1536]{1,0:T(8,128)} %bitcast.259, s32[4096]{0:T(1024)S(1)} %copy-done.10), kind=kCustom, calls=%fused_computation.4 | custom fusion | bytes 50348032 | tf_op jit(solution)/shard_map/gather | solution.py:288
  624.3 28.9 %reshape.829 = f32[1024,4,1536]{2,1,0:T(4,128)} reshape(f32[4096,1536]{1,0:T(8,128)} %gather_fusion.4) | data formatting | bytes 50331648 | tf_op jit(solution)/shard_map/gather | solution.py:288
  653.2 55.7 %fusion.18 = f32[1024,1,4]{2,1,0:T(1,128)} fusion(f32[1024,4,1536]{2,1,0:T(4,128)} %reshape.829, bf16[1024,1536,1]{1,0,2:T(8,128)(2,1)S(1)} %bitcast.258), kind=kOutput, calls=%fused_computation.48 | convolution fusion | flops 75497472 | bytes 28327936 | tf_op jit(solution)/shard_map/td,tkd->tk/dot_general | solution.py:304
  710.0 8.1 psum.21
  719.3 23.2 %gather_fusion.5 = f32[4096]{0:T(1024)S(1)} fusion(f32[4096]{0:T(1024)S(1)} %and_select_fusion.1, s32[4096]{0:T(1024)S(1)} %copy-done.79), kind=kCustom, calls=%fused_computation.5 | custom fusion | bytes 49152 | tf_op jit(solution)/shard_map/gather | solution.py:298
  742.6 18.9 multiply_convert_fusion.1
  761.5 16.7 fusion.152
  778.2 23.7 %convolution_add_fusion = f32[8,512,1536]{2,1,0:T(8,128)} fusion(f32[8,512,1536]{2,1,0:T(8,128)} %fusion.152, bf16[8,512,384]{2,1,0:T(8,128)(2,1)} %get-tuple-element.165, bf16[8,1536,384]{2,1,0:T(8,128)(2,1)} %all-gather.21.cloned.1.call-done), kind=kOutput, calls=%fused_computation.14 | convolution fusion | flops 4838129664 | bytes 62914560 | tf_op jit(solution)/shard_map/ecf,edf->ecd/dot_general | solution.py:323
  801.9 35.4 %gather_fusion.7 = f32[4096,1536]{1,0:T(8,128)} fusion(f32[4096,1536]{1,0:T(8,128)} %bitcast.260, s32[4096]{0:T(1024)S(1)} %copy-done.10), kind=kCustom, calls=%fused_computation.7 | custom fusion | bytes 50348032 | tf_op jit(solution)/shard_map/gather | solution.py:328
  837.2 28.8 %reshape.853 = f32[1024,4,1536]{2,1,0:T(4,128)} reshape(f32[4096,1536]{1,0:T(8,128)} %gather_fusion.7) | data formatting | bytes 50331648 | tf_op jit(solution)/shard_map/gather | solution.py:328
  866.1 63.6 %multiply_reduce_fusion = bf16[1024,1536]{1,0:T(8,128)(2,1)} fusion(f32[1024,4,1536]{2,1,0:T(4,128)} %reshape.853, f32[1024,4]{1,0:T(8,128)S(1)} %copy-done.36), kind=kLoop, calls=%fused_computation.11 | loop fusion | flops 11010048 | bytes 28327936 | tf_op jit(solution)/shard_map/reduce_sum | solution.py:328
  930.6 63.3 %multiply_reduce_fusion.1 = bf16[1024,1536]{1,0:T(8,128)(2,1)} fusion(f32[1024,4,1536]{2,1,0:T(4,128)} %reshape.829, f32[1024,4]{1,0:T(8,128)S(1)} %copy.178), kind=kLoop, calls=%fused_computation.13 | loop fusion | flops 11010048 | bytes 28327936 | tf_op jit(solution)/shard_map/reduce_sum | solution.py:289
  995.8 5.1 multiply_reduce_fusion.2
  1000.9 33.8 %reduce-scatter.17.cloned.1.call-done = bf16[512,1536]{1,0:T(8,128)(2,1)} async-done(((bf16[1024,1536]{1,0:T(8,128)(2,1)}), bf16[512,1536]{1,0:T(8,128)(2,1)}) %reduce-scatter.17.cloned.1.call-update) | async-done | bytes 1572880 | tf_op jit(solution)/shard_map/reduce_scatter | solution.py:290
  1034.8 6.4 fusion.140
  1043.8 42.5 %all-gather.27.cloned.1.call-done = bf16[1024,1536]{1,0:T(8,128)(2,1)} async-done(((bf16[512,1536]{1,0:T(8,128)(2,1)}), bf16[1024,1536]{1,0:T(8,128)(2,1)}) %all-gather.27.cloned.1.call-update) | async-done | bytes 3145744 | tf_op jit(solution)/shard_map/all_gather | solution.py:339
  1086.3 5.3 convolution_convert_fusion.1
  1092.6 7.4 fusion.13
  1100.0 4.8 fusion.72
  1104.8 4.9 fusion.35
  1114.2 6.1 fusion
  1120.3 6.8 fusion.12
  1154.9 6.0 fusion.155
  1162.3 6.8 fusion.157
  1171.0 15.6 fusion.28
  1188.4 13.3 fusion.6
  1203.6 13.4 fusion.5
  1222.1 61.5 %all-reduce.6 = (f32[1536]{0:T(1024)S(1)}, f32[1536]{0:T(1024)S(1)}) all-reduce(f32[1536]{0:T(1024)S(1)} %get-tuple-element.149, f32[1536]{0:T(1024)S(1)} %copy-done.93), channel_id=6, replica_groups=mesh['dp'=16,'tensor'=2] {'dp'}, use_global_device_ids=true, to_apply=%region_27.28.clone | all-reduce | flops 3072 | bytes 24576
  1283.8 5.4 all-reduce.7
  1289.2 4.5 fusion.31
  1293.7 18.7 reduce-scatter.27.cloned.1.call-done
  1312.4 79.3 %reduce-scatter.23.cloned.1.call-done = f32[96,768]{1,0:T(8,128)} async-done(((f32[1536,768]{1,0:T(8,128)}), f32[96,768]{1,0:T(8,128)}) %reduce-scatter.23.cloned.1.call-update) | async-done | bytes 294928 | tf_op jit(solution)/shard_map/reduce_scatter | solution.py:385
  1391.7 78.9 %reduce-scatter.29.cloned.1.call-done = f32[96,768]{1,0:T(8,128)} async-done(((f32[1536,768]{1,0:T(8,128)}), f32[96,768]{1,0:T(8,128)}) %reduce-scatter.29.cloned.1.call-update) | async-done | bytes 294928 | tf_op jit(solution)/shard_map/reduce_scatter | solution.py:388
  1470.7 199.3 %reduce-scatter.35.cloned.1.call-done = f32[8,96,384]{2,1,0:T(8,128)} async-done(((f32[8,1536,384]{2,1,0:T(8,128)}), f32[8,96,384]{2,1,0:T(8,128)}) %reduce-scatter.35.cloned.1.call-update) | async-done | bytes 1179664 | tf_op jit(solution)/shard_map/reduce_scatter | solution.py:393
  1669.9 199.0 %reduce-scatter.31.cloned.1.call-done = f32[8,96,384]{2,1,0:T(8,128)} async-done(((f32[8,1536,384]{2,1,0:T(8,128)}), f32[8,96,384]{2,1,0:T(8,128)}) %reduce-scatter.31.cloned.1.call-update) | async-done | bytes 1179664 | tf_op jit(solution)/shard_map/reduce_scatter | solution.py:391
  1868.9 199.2 %reduce-scatter.33.cloned.1.call-done = f32[8,96,384]{2,1,0:T(8,128)} async-done(((f32[8,1536,384]{2,1,0:T(8,128)}), f32[8,96,384]{2,1,0:T(8,128)}) %reduce-scatter.33.cloned.1.call-update) | async-done | bytes 1179664 | tf_op jit(solution)/shard_map/reduce_scatter | solution.py:392
  (377 shorter events, 106.6 us)
Async XLA Ops:
  7.2 93.3 %all-gather.11.cloned.1.call-start = ((), (), s32[]{:S(2)}) async-start(), calls=%async_computation.12 | async-start | bytes 4718592 | tf_op jit(solution)/shard_map/all_gather | solution.py:233
  46.9 7.6 copy-start.82
  46.9 26.5 %copy-start.83 = (bf16[96,128]{1,0:T(8,128)(2,1)S(1)}, bf16[96,128]{1,0:T(8,128)(2,1)}, u32[]{:S(2)}) copy-start(bf16[96,128]{1,0:T(8,128)(2,1)} %param.33) | copy-start | bytes 73732
  52.9 86.9 %all-gather.13.cloned.1.call-start = ((), (), s32[]{:S(2)}) async-start(), calls=%async_computation.13 | async-start | bytes 2506752 | tf_op jit(solution)/shard_map/all_gather | solution.py:110
  53.7 129.4 %all-gather.15.cloned.1.call-start = ((), (), s32[]{:S(2)}) async-start(), calls=%async_computation.14 | async-start | bytes 2506752 | tf_op jit(solution)/shard_map/all_gather | solution.py:113
  54.4 176.7 %reduce-scatter.15.cloned.1.call-start = ((), (), s32[]{:S(2)}) async-start(), calls=%async_computation.15 | async-start | bytes 4718592 | tf_op jit(solution)/shard_map/reduce_scatter | solution.py:262
  54.5 49.2 %copy-start.70 = (f32[1024]{0:T(1024)}, f32[1024]{0:T(1024)S(1)}, u32[]{:S(2)}) copy-start(f32[1024]{0:T(1024)S(1)} %fusion.123) | copy-start | bytes 12292
  54.5 49.2 %copy-start.95 = (f32[64]{0:T(128)}, f32[64]{0:T(128)S(1)}, u32[]{:S(2)}) copy-start(f32[64]{0:T(128)S(1)} %multiply_power_fusion) | copy-start | bytes 772
  72.8 30.9 %copy-start.30 = (bf16[1536,128]{1,0:T(8,128)(2,1)}, bf16[1536,128]{1,0:T(8,128)(2,1)S(1)}, u32[]{:S(2)}) copy-start(bf16[1536,128]{1,0:T(8,128)(2,1)S(1)} %all_gather.45) | copy-start | bytes 1179652
  95.3 93.8 %copy-start.86 = (f32[512]{0:T(512)}, f32[512]{0:T(512)S(1)}, u32[]{:S(2)}) copy-start(f32[512]{0:T(512)S(1)} %get-tuple-element.192) | copy-start | bytes 6148
  107.5 57.8 %copy-start.45 = (bf16[1024,128]{1,0:T(8,128)(2,1)}, bf16[1024,128]{1,0:T(8,128)(2,1)S(1)}, u32[]{:S(2)}) copy-start(bf16[1024,128]{1,0:T(8,128)(2,1)S(1)} %convolution_convert_fusion.2) | copy-start | bytes 786436
  156.8 7.2 copy-start.6
  156.8 7.2 copy-start.56
  169.8 19.1 copy-start.38
  188.9 42.3 %copy-start.7 = (bf16[512,1536]{1,0:T(8,128)(2,1)S(1)}, bf16[512,1536]{1,0:T(8,128)(2,1)}, u32[]{:S(2)}) copy-start(bf16[512,1536]{1,0:T(8,128)(2,1)} %param.27) | copy-start | bytes 4718596
  188.9 182.4 %all-gather.25.cloned.1.call-start = ((), (), s32[]{:S(2)}) async-start(), calls=%async_computation.21 | async-start | bytes 4718592 | tf_op jit(solution)/shard_map/all_gather | solution.py:296
  191.7 225.0 %all-gather.17.cloned.1.call-start = ((), (), s32[]{:S(2)}) async-start(), calls=%async_computation.16 | async-start | bytes 4718592 | tf_op jit(solution)/shard_map/all_gather | solution.py:267
  191.8 44.4 %copy-start.68 = (f32[1536]{0:T(1024)}, f32[1536]{0:T(1024)S(1)}, u32[]{:S(2)}) copy-start(f32[1536]{0:T(1024)S(1)} %convert_element_type.201) | copy-start | bytes 18436
  236.2 252.3 %all-gather.19.cloned.1.call-start = ((), (), s32[]{:S(2)}) async-start(), calls=%async_computation.17 | async-start | bytes 10027008 | tf_op jit(solution)/shard_map/all_gather | solution.py:119
  237.0 265.7 %all-gather.21.cloned.1.call-start = ((), (), s32[]{:S(2)}) async-start(), calls=%async_computation.18 | async-start | bytes 10027008 | tf_op jit(solution)/shard_map/all_gather | solution.py:120
  237.7 335.4 %all-gather.23.cloned.1.call-start = ((), (), s32[]{:S(2)}) async-start(), calls=%async_computation.19 | async-start | bytes 10027008 | tf_op jit(solution)/shard_map/all_gather | solution.py:121
  238.5 755.6 %reduce-scatter.19.cloned.1.call-start = ((), (), s32[]{:S(2)}) async-start(), calls=%async_computation.22 | async-start | bytes 4718592 | tf_op jit(solution)/shard_map/reduce_scatter | solution.py:329
  239.6 39.1 %copy-start = (s32[4096]{0:T(1024)}, s32[4096]{0:T(1024)S(1)}, u32[]{:S(2)}) copy-start(s32[4096]{0:T(1024)S(1)} %reshape.782) | copy-start | bytes 49156
  327.9 40.6 %copy-start.54 = (s32[4096]{0:T(1024)}, s32[4096]{0:T(1024)S(1)}, u32[]{:S(2)}) copy-start(s32[4096]{0:T(1024)S(1)} %gather_fusion.2) | copy-start | bytes 49156
  327.9 18.7 copy-start.98
  368.5 93.8 %copy-start.66 = (bf16[1536,8]{0,1:T(8,128)(2,1)}, bf16[1536,8]{0,1:T(8,128)(2,1)S(1)}, u32[]{:S(2)}) copy-start(bf16[1536,8]{0,1:T(8,128)(2,1)S(1)} %reshape.903) | copy-start | bytes 73732
  444.5 17.7 copy-start.2
  463.2 25.3 %copy-start.51 = (s32[1024,4]{0,1:T(4,128)S(1)}, s32[1024,4]{0,1:T(4,128)}, u32[]{:S(2)}) copy-start(s32[1024,4]{0,1:T(4,128)} %param.39) | copy-start | bytes 49156
  463.2 25.4 %copy-start.90 = (pred[8,512]{1,0:T(8,128)(4,1)S(1)}, pred[8,512]{1,0:T(8,128)(4,1)}, u32[]{:S(2)}) copy-start(pred[8,512]{1,0:T(8,128)(4,1)} %lt.138) | copy-start | bytes 12292
  518.1 70.9 %copy-start.13 = (bf16[8,512,384]{2,1,0:T(8,128)(2,1)}, bf16[8,512,384]{2,1,0:T(8,128)(2,1)S(1)}, u32[]{:S(2)}) copy-start(bf16[8,512,384]{2,1,0:T(8,128)(2,1)S(1)} %get-tuple-element.200) | copy-start | bytes 9437188
  573.2 15.8 copy-start.10
  624.3 28.9 %copy-start.4 = (bf16[1024,1536]{1,0:T(8,128)(2,1)S(1)}, bf16[1024,1536]{1,0:T(8,128)(2,1)}, u32[]{:S(2)}) copy-start(bf16[1024,1536]{1,0:T(8,128)(2,1)} %all-gather.25.cloned.1.call-done) | copy-start | bytes 9437188
  653.1 65.0 %copy-start.77 = (pred[1024,4]{0,1:T(4,128)(4,1)S(1)}, pred[1024,4]{0,1:T(4,128)(4,1)}, u32[]{:S(2)}) copy-start(pred[1024,4]{0,1:T(4,128)(4,1)} %copy-done.76) | copy-start | bytes 12292
  653.1 66.2 %copy-start.1 = (s32[4096]{0:T(1024)S(1)}, s32[4096]{0:T(1024)}, u32[]{:S(2)}) copy-start(s32[4096]{0:T(1024)} %copy-done) | copy-start | bytes 49156
  653.2 66.2 %copy-start.55 = (s32[4096]{0:T(1024)S(1)}, s32[4096]{0:T(1024)}, u32[]{:S(2)}) copy-start(s32[4096]{0:T(1024)} %copy-done.54) | copy-start | bytes 49156
  653.2 66.2 %copy-start.79 = (s32[4096]{0:T(1024)S(1)}, s32[4096]{0:T(1024)}, u32[]{:S(2)}) copy-start(s32[4096]{0:T(1024)} %get-tuple-element.182) | copy-start | bytes 49156
  718.8 23.8 %copy-start.58 = (f32[1024,4]{0,1:T(4,128)}, f32[1024,4]{0,1:T(4,128)S(1)}, u32[]{:S(2)}) copy-start(f32[1024,4]{0,1:T(4,128)S(1)} %get-tuple-element.160) | copy-start | bytes 49156
  742.6 18.9 copy-start.48
  761.5 16.7 copy-start.20
  837.2 28.9 %copy-start.36 = (f32[1024,4]{1,0:T(8,128)S(1)}, f32[1024,4]{1,0:T(8,128)}, u32[]{:S(2)}) copy-start(f32[1024,4]{1,0:T(8,128)} %copy.186) | copy-start | bytes 49156
  929.7 105.1 %reduce-scatter.17.cloned.1.call-start = ((), (), s32[]{:S(2)}) async-start(), calls=%async_computation.20 | async-start | bytes 4718592 | tf_op jit(solution)/shard_map/reduce_scatter | solution.py:290
  930.6 63.4 %copy-start.52 = (s32[1024,4]{0,1:T(4,128)S(1)}, s32[1024,4]{0,1:T(4,128)}, u32[]{:S(2)}) copy-start(s32[1024,4]{0,1:T(4,128)} %param.39) | copy-start | bytes 49156
  994.0 92.4 %all-gather.27.cloned.1.call-start = ((), (), s32[]{:S(2)}) async-start(), calls=%async_computation.23 | async-start | bytes 4718592 | tf_op jit(solution)/shard_map/all_gather | solution.py:339
  994.1 40.7 %copy-start.87 = (f32[512]{0:T(512)S(1)}, f32[512]{0:T(512)}, u32[]{:S(2)}) copy-start(f32[512]{0:T(512)} %copy-done.86) | copy-start | bytes 6148
  994.1 40.7 %copy-start.92 = (f32[512]{0:T(512)S(1)}, f32[512]{0:T(512)}, u32[]{:S(2)}) copy-start(f32[512]{0:T(512)} %get-tuple-element.190) | copy-start | bytes 6148
  1034.8 7.0 copy-start.63
  1034.8 7.0 copy-start.3
  1041.3 176.6 %reduce-scatter.37.cloned.1.call-start = ((), (), s32[]{:S(2)}) async-start(), calls=%async_computation.32 | async-start | bytes 835584
  1041.8 58.2 %copy-start.53 = (f32[6,512]{1,0:T(8,128)}, f32[6,512]{1,0:T(8,128)S(1)}, u32[]{:S(2)}) copy-start(f32[6,512]{1,0:T(8,128)S(1)} %log_add_fusion.1) | copy-start | bytes 36868
  1043.8 175.6 %reduce-scatter.21.cloned.1.call-start = ((), (), s32[]{:S(2)}) async-start(), calls=%async_computation.24 | async-start | bytes 4718592 | tf_op jit(solution)/shard_map/reduce_scatter | solution.py:374
  1092.6 12.2 slice-start.3
  1092.6 12.2 slice-start.4
  1104.8 9.3 slice-start
  1104.8 9.3 slice-start.1
  1133.2 7.3 copy-start.42
  1148.1 145.5 %reduce-scatter.25.cloned.1.call-start = ((), (), s32[]{:S(2)}) async-start(), calls=%async_computation.26 | async-start | bytes 835584 | tf_op jit(solution)/shard_map/reduce_scatter | solution.py:386
  1152.9 159.5 %reduce-scatter.27.cloned.1.call-start = ((), (), s32[]{:S(2)}) async-start(), calls=%async_computation.27 | async-start | bytes 835584 | tf_op jit(solution)/shard_map/reduce_scatter | solution.py:387
  1154.9 236.9 %reduce-scatter.23.cloned.1.call-start = ((), (), s32[]{:S(2)}) async-start(), calls=%async_computation.25 | async-start | bytes 5013504 | tf_op jit(solution)/shard_map/reduce_scatter | solution.py:385
  1160.9 309.7 %reduce-scatter.29.cloned.1.call-start = ((), (), s32[]{:S(2)}) async-start(), calls=%async_computation.28 | async-start | bytes 5013504 | tf_op jit(solution)/shard_map/reduce_scatter | solution.py:388
  1169.1 500.8 %reduce-scatter.35.cloned.1.call-start = ((), (), s32[]{:S(2)}) async-start(), calls=%async_computation.31 | async-start | bytes 20054016 | tf_op jit(solution)/shard_map/reduce_scatter | solution.py:393
  1186.6 682.3 %reduce-scatter.31.cloned.1.call-start = ((), (), s32[]{:S(2)}) async-start(), calls=%async_computation.29 | async-start | bytes 20054016 | tf_op jit(solution)/shard_map/reduce_scatter | solution.py:391
  1201.7 866.3 %reduce-scatter.33.cloned.1.call-start = ((), (), s32[]{:S(2)}) async-start(), calls=%async_computation.30 | async-start | bytes 20054016 | tf_op jit(solution)/shard_map/reduce_scatter | solution.py:392
  1217.1 72.1 %copy-start.94 = (f32[512]{0:T(512)S(1)}, f32[512]{0:T(512)}, u32[]{:S(2)}) copy-start(f32[512]{0:T(512)} %get-tuple-element.188) | copy-start | bytes 6148
  1219.4 69.8 %copy-start.26 = (bf16[512,1536]{1,0:T(8,128)(2,1)S(1)}, bf16[512,1536]{1,0:T(8,128)(2,1)}, u32[]{:S(2)}) copy-start(bf16[512,1536]{1,0:T(8,128)(2,1)} %reduce-scatter.21.cloned.1.call-done) | copy-start | bytes 4718596
  (62 other events, 159.7 us)
Sparse Core Ops, SparseCore 0:
  53.1 42.1 all-gather.10
  97.6 42.1 all-gather.12
  142.1 40.9 all-gather.14
  189.0 42.1 reduce-scatter.14
  232.6 44.9 all-gather.24
  279.7 44.9 all-gather.16
  327.2 81.5 all-gather.18
  411.3 79.5 all-gather.20
  493.5 79.5 all-gather.22
  929.8 40.6 reduce-scatter.18
  994.1 40.6 reduce-scatter.16
  1041.4 44.9 all-gather.26
  1090.3 56.5 reduce-scatter.36
  1149.0 42.6 reduce-scatter.20
  1196.1 56.6 reduce-scatter.24
  1256.8 55.5 reduce-scatter.26
  1317.2 74.5 reduce-scatter.22
  1396.0 74.5 reduce-scatter.28
  1475.9 193.9 reduce-scatter.34
  1675.0 193.8 reduce-scatter.30
  1874.2 193.8 reduce-scatter.32
where the time goes:
time: 2080 us
  waiting for transfers between devices  995 us (48%)
  local copies, waits for them, and re-layouts  410 us (20%)
  matrix products  293 us (14%)
  other arithmetic  185 us (9%)
  blocking collectives  173 us (8%)
    reduce_scatter x1, waiting for transfers between devices, shards(): lax.psum_scatter(down_w_grad, 'dp', scatter_dimension=1, tiled=True)  199 us
    reduce_scatter x1, waiting for transfers between devices, shards(): lax.psum_scatter(up_w_grad, 'dp', scatter_dimension=1, tiled=True)  199 us
    reduce_scatter x1, waiting for transfers between devices, shards(): lax.psum_scatter(gate_w_grad, 'dp', scatter_dimension=1, tiled=True)  199 us
    unnamed x2, blocking collectives  97.5 us
    reduce_scatter x1, waiting for transfers between devices, shards(): lax.psum_scatter(query_w_grad, 'dp', scatter_dimension=0, tiled=True)  79.3 us
    reduce_scatter x1, waiting for transfers between devices, shards(): lax.psum_scatter(out_grad, 'dp', scatter_dimension=0, tiled=True)  78.9 us
    gather x2, local copies, waits for them, and re-layouts, shards(): expert_in_grad[slot_rows]  64.2 us
    gather x2, local copies, waits for them, and re-layouts, shards(): picked = expert_out[slot_rows]  64.1 us
  transfers between devices with their start and end apart: 21, of which 12 were waited for; matrix products, arithmetic and copies ran while one was open for 24% of the time, Pallas kernels for 0%

commit v1 on v0

v1 whole, which is shorter than its diff:
```python
import functools

import jax
import jax.numpy as jnp
from jax import lax
from jax.experimental import pallas as pl
from jax.experimental.pallas import tpu as pltpu
from jax.sharding import PartitionSpec as P

WIDTH = 1536
HEADS = 12
KV_HEADS = 2
HEAD = 128
FF = 768
TOP = 4
EXPERTS = 8
GROUP = 1024
CAP = 512
EPSILON = 1e-06
ROPE_BASE = 10000.0
F32 = jnp.float32
BF16 = jnp.bfloat16
LANES = 128
ROWS = 256
SCALE = HEAD ** (-0.5)
VMEM_LIMIT = 60 * 1024 * 1024


def dot(left, right):
    return jnp.dot(left, right, preferred_element_type=F32)


def dot_nt(left, right):
    return lax.dot_general(left, right, (((1,), (1,)), ((), ())), preferred_element_type=F32)


def params(**kw):
    return pltpu.CompilerParams(vmem_limit_bytes=VMEM_LIMIT, **kw)


def whole(shape):
    zeros = (0,) * len(shape)
    return pl.BlockSpec(shape, lambda *_: zeros)


def once(shape):
    zeros = (0,) * len(shape)
    return pl.BlockSpec(shape, lambda *_: zeros, pipeline_mode=pl.Buffered(1))


def route_kernel(length_ref, routes_ref, priority_ref, member_ref, keep_ref):
    expert = lax.broadcasted_iota(jnp.int32, (EXPERTS, GROUP), 0)
    place = lax.broadcasted_iota(jnp.int32, (EXPERTS, GROUP), 1)
    order = jnp.full((EXPERTS, GROUP), 1 << 20, jnp.int32)
    for j in range(TOP):
        order = jnp.where(routes_ref[j : j + 1, :] == expert, priority_ref[j : j + 1, :], order)
    member = order < (1 << 19)
    order = jnp.where(place < length_ref[0], order, 1 << 20)
    bound = jnp.zeros((EXPERTS, 1), jnp.int32)
    for bit in range(12, -1, -1):
        trial = bound + (1 << bit)
        count = jnp.sum((order < trial).astype(F32), axis=1, keepdims=True)
        bound = jnp.where(count <= CAP, trial, bound)
    member_ref[...] = member.astype(F32)
    keep_ref[...] = (order < bound).astype(F32)


def route(length, routes, priority):
    return pl.pallas_call(
        route_kernel,
        name="route",
        out_shape=(jax.ShapeDtypeStruct((EXPERTS, GROUP), F32),) * 2,
        in_specs=[
            pl.BlockSpec(memory_space=pltpu.SMEM),
            pl.BlockSpec(memory_space=pltpu.VMEM),
            pl.BlockSpec(memory_space=pltpu.VMEM),
        ],
        out_specs=(pl.BlockSpec(memory_space=pltpu.VMEM),) * 2,
    )(length, routes.T, priority.T)


def rope(v, cos, sin):
    return v * cos + pltpu.roll(v, HEAD // 2, 1) * sin


def qkv_kernel(x_ref, gain_ref, w_ref, cos_ref, sin_ref, xnt_ref, q_ref, k_ref, v_ref):
    x = x_ref[...].astype(F32)
    scale = lax.rsqrt(jnp.mean(x * x, axis=1, keepdims=True) + EPSILON)
    xn = (x * scale * gain_ref[...]).astype(BF16)
    xnt_ref[...] = xn.T
    cos, sin = cos_ref[...], sin_ref[...]
    q_width = q_ref.shape[1]
    out = dot(xn, w_ref[:, : q_width + 2 * HEAD])
    for h in range(q_width // HEAD):
        cols = slice(h * HEAD, (h + 1) * HEAD)
        q_ref[:, cols] = rope(out[:, cols], cos, sin).astype(BF16)
    k_ref[...] = rope(out[:, q_width : q_width + HEAD], cos, sin).astype(BF16)
    v_ref[...] = out[:, q_width + HEAD :].astype(BF16)


def qkv(x, gain, weights, cos, sin, q_width):
    rows = lambda width: pl.BlockSpec((ROWS, width), lambda i: (i, 0))
    return pl.pallas_call(
        qkv_kernel,
        name="qkv",
        grid=(GROUP // ROWS,),
        out_shape=(
            jax.ShapeDtypeStruct((WIDTH, GROUP), BF16),
            jax.ShapeDtypeStruct((GROUP, q_width), BF16),
            jax.ShapeDtypeStruct((GROUP, HEAD), BF16),
            jax.ShapeDtypeStruct((GROUP, HEAD), BF16),
        ),
        in_specs=[
            rows(WIDTH),
            whole((1, WIDTH)),
            whole(weights.shape),
            rows(HEAD),
            rows(HEAD),
        ],
        out_specs=(
            pl.BlockSpec((WIDTH, ROWS), lambda i: (0, i)),
            rows(q_width),
            rows(HEAD),
            rows(HEAD),
        ),
        compiler_params=params(),
    )(x, gain, weights, cos, sin)


def scores_t(k, q, first_row, length):
    s = dot_nt(k, q) * SCALE
    key = lax.broadcasted_iota(jnp.int32, s.shape, 0)
    query = lax.broadcasted_iota(jnp.int32, (1, s.shape[1]), 1) + first_row
    return jnp.where(key < jnp.minimum(query + 1, length), s, -1e30)


def attend_kernel(half, length_ref, q_ref, k_ref, v_ref, o_ref, lse_ref):
    length = length_ref[0]
    vt = v_ref[...].T
    heads = q_ref.shape[1] // HEAD
    for block in range(q_ref.shape[0] // ROWS):
        first = half * q_ref.shape[0] + block * ROWS
        keys = first + ROWS
        rows = slice(block * ROWS, (block + 1) * ROWS)
        for h in range(heads):
            cols = slice(h * HEAD, (h + 1) * HEAD)
            s = scores_t(k_ref[:keys, :], q_ref[rows, cols], first, length)
            peak = jnp.max(s, axis=0, keepdims=True)
            e = jnp.exp(s - peak)
            total = jnp.sum(e, axis=0, keepdims=True)
            p = (e * (1.0 / total)).astype(BF16)
            ot = dot(vt[:, :keys], p)
            o_ref[rows, cols] = ot.T.astype(BF16)
            lse_ref[h : h + 1, rows] = peak + jnp.log(total)


def attend(half, halves, length, q, k, v):
    count = GROUP // halves
    q_width = q.shape[1]
    return pl.pallas_call(
        functools.partial(attend_kernel, half),
        name="attend",
        grid=(1,),
        out_shape=(
            jax.ShapeDtypeStruct((count, q_width), BF16),
            jax.ShapeDtypeStruct((8, count), F32),
        ),
        in_specs=[
            pl.BlockSpec(memory_space=pltpu.SMEM),
            pl.BlockSpec((count, q_width), lambda i: (half, 0)),
            whole((GROUP, HEAD)),
            whole((GROUP, HEAD)),
        ],
        out_specs=(whole((count, q_width)), whole((8, count))),
        compiler_params=params(),
    )(length, q, k, v)


def attend_back_kernel(
    length_ref, g_ref, wo_ref, q_ref, k_ref, v_ref, lse_ref, cos_ref, sin_ref, out_ref, do_ref
):
    length = length_ref[0]
    heads = q_ref.shape[1] // HEAD
    width = q_ref.shape[1]
    for block in range(GROUP // ROWS):
        rows = slice(block * ROWS, (block + 1) * ROWS)
        do_ref[rows, :] = dot(g_ref[rows, :], wo_ref[:, :width]).astype(BF16)
    kt = k_ref[...].T
    dk = [jnp.zeros((ROWS, HEAD), F32) for _ in range(GROUP // ROWS)]
    dv = [jnp.zeros((ROWS, HEAD), F32) for _ in range(GROUP // ROWS)]
    for block in range(GROUP // ROWS):
        first = block * ROWS
        keys = first + ROWS
        rows = slice(first, keys)
        cos, sin = cos_ref[rows, :], sin_ref[rows, :]
        dk_sum = jnp.zeros((keys, HEAD), F32)
        dv_sum = jnp.zeros((keys, HEAD), F32)
        for h in range(heads):
            cols = slice(h * HEAD, (h + 1) * HEAD)
            q, do = q_ref[rows, cols], do_ref[rows, cols]
            s = scores_t(k_ref[:keys, :], q, first, length)
            p = jnp.exp(s - lse_ref[h : h + 1, rows])
            dp = dot_nt(v_ref[:keys, :], do)
            inner = jnp.sum(p * dp, axis=0, keepdims=True)
            ds = (p * (dp - inner)).astype(BF16)
            dv_sum += dot(p.astype(BF16), do)
            dk_sum += dot(ds, q)
            dq = dot(kt[:, :keys], ds).T * SCALE
            out_ref[rows, cols] = rope(dq, cos, -sin).astype(BF16)
        for j in range(block + 1):
            part = slice(j * ROWS, (j + 1) * ROWS)
            dk[j] += dk_sum[part]
            dv[j] += dv_sum[part]
    for block in range(GROUP // ROWS):
        rows = slice(block * ROWS, (block + 1) * ROWS)
        out_ref[rows, width : width + HEAD] = rope(
            dk[block] * SCALE, cos_ref[rows, :], -sin_ref[rows, :]
        ).astype(BF16)
        out_ref[rows, width + HEAD :] = dv[block].astype(BF16)


def attend_back(length, grad, wo, q, k, v, lse, cos, sin):
    q_width = q.shape[1]
    return pl.pallas_call(
        attend_back_kernel,
        name="attend_back",
        grid=(1,),
        out_shape=jax.ShapeDtypeStruct((GROUP, q_width + 2 * HEAD), BF16),
        in_specs=[
            pl.BlockSpec(memory_space=pltpu.SMEM),
            whole((GROUP, WIDTH)),
            whole(wo.shape),
            whole((GROUP, q_width)),
            whole((GROUP, HEAD)),
            whole((GROUP, HEAD)),
            whole((8, GROUP)),
            whole((GROUP, HEAD)),
            whole((GROUP, HEAD)),
        ],
        out_specs=whole((GROUP, q_width + 2 * HEAD)),
        scratch_shapes=[pltpu.VMEM((GROUP, q_width), BF16)],
        compiler_params=params(),
    )(length, grad, wo, q, k, v, lse, cos, sin)


def out_kernel(x_ref, oa_ref, ob_ref, wo_ref, gain_ref, r_ref, member_ref, keep_ref,
               h_ref, u_ref, ut_ref, gate_ref, weight_ref):
    width = oa_ref.shape[1]
    h = (
        dot_nt(oa_ref[...], wo_ref[:, :width]) + dot_nt(ob_ref[...], wo_ref[:, width:])
    ) + x_ref[...].astype(F32)
    h_ref[...] = h
    scale = lax.rsqrt(jnp.mean(h * h, axis=1, keepdims=True) + EPSILON)
    u = (h * scale * gain_ref[...]).astype(BF16)
    u_ref[...] = u
    ut_ref[...] = u.T
    z = dot(u, r_ref[...])
    member = member_ref[...] > 0
    peak = jnp.max(jnp.where(member, z, -1e30), axis=1, keepdims=True)
    e = jnp.where(member, jnp.exp(jnp.where(member, z - peak, 0.0)), 0.0)
    gate = e / jnp.sum(e, axis=1, keepdims=True)
    gate_ref[...] = gate
    weight_ref[...] = gate * keep_ref[...]


def out_project(half, halves, x, oa, ob, wo, gain, router, member, keep):
    count = GROUP // halves
    blocks = count // ROWS
    first = half * blocks
    local = lambda width: pl.BlockSpec((ROWS, width), lambda i: (i, 0))
    full = lambda width: pl.BlockSpec((ROWS, width), lambda i: (i + first, 0))
    return pl.pallas_call(
        out_kernel,
        name="out_project",
        grid=(blocks,),
        out_shape=(
            jax.ShapeDtypeStruct((count, WIDTH), F32),
            jax.ShapeDtypeStruct((count, WIDTH), BF16),
            jax.ShapeDtypeStruct((WIDTH, count), BF16),
            jax.ShapeDtypeStruct((count, LANES), F32),
            jax.ShapeDtypeStruct((count, LANES), F32),
        ),
        in_specs=[
            full(WIDTH),
            local(oa.shape[1]),
            local(ob.shape[1]),
            whole(wo.shape),
            whole((1, WIDTH)),
            whole((WIDTH, LANES)),
            full(LANES),
            full(LANES),
        ],
        out_specs=(
            local(WIDTH),
            local(WIDTH),
            pl.BlockSpec((WIDTH, ROWS), lambda i: (0, i)),
            local(LANES),
            local(LANES),
        ),
        compiler_params=params(),
    )(x, oa, ob, wo, gain, router, member, keep)


def experts_kernel(first_pair, chained, *refs):
    if chained:
        u_ref, g_ref, ut_ref, gt_ref, w_ref, weight_ref, f_in, du_in, dg_in = refs[:9]
        rest = refs[9:]
    else:
        u_ref, g_ref, ut_ref, gt_ref, w_ref, weight_ref = refs[:6]
        rest = refs[6:]
    dw_ref, f_ref, du_ref, dg_ref, f_acc, du_acc, dg_acc, dab, wh = rest
    pair, step = pl.program_id(0), pl.program_id(1)
    part = w_ref.shape[2] // 6
    blocks = GROUP // ROWS

    @pl.when(step < blocks)
    def _():
        rows = pl.ds(pl.multiple_of(step * ROWS, ROWS), ROWS)
        ab = dot(u_ref[...], w_ref[0, :, : 4 * part])
        d = dot(g_ref[...], w_ref[0, :, 4 * part :])
        lane = lax.broadcasted_iota(jnp.int32, (ROWS, LANES), 1)
        weights = weight_ref[...]
        fresh = pair == 0
        if chained:
            dg = jnp.where(fresh, dg_in[...], dg_acc[rows, :])
        else:
            dg = jnp.where(fresh, 0.0, dg_acc[rows, :])
        for i in range(2):
            mine = lane == 2 * (first_pair + pair) + i
            w = jnp.sum(jnp.where(mine, weights, 0.0), axis=1, keepdims=True)
            a = ab[:, 2 * i * part : (2 * i + 1) * part]
            b = ab[:, (2 * i + 1) * part : (2 * i + 2) * part]
            dh = d[:, i * part : (i + 1) * part]
            s = 1.0 / (1.0 + jnp.exp(-a))
            act = a * s
            hid = (act * b).astype(BF16).astype(F32)
            dg += jnp.where(mine, jnp.sum(hid * dh, axis=1, keepdims=True), 0.0)
            wh[rows, i * part : (i + 1) * part] = (w * hid).astype(BF16)
            dh = dh * w
            dab[rows, 2 * i * part : (2 * i + 1) * part] = (
                dh * b * (s * (1.0 + a * (1.0 - s)))
            ).astype(BF16)
            dab[rows, (2 * i + 1) * part : (2 * i + 2) * part] = (dh * act).astype(BF16)
        dg_acc[rows, :] = dg
        dg_ref[...] = dg
        f = dot_nt(wh[rows, :], w_ref[0, :, 4 * part :])
        du = dot_nt(dab[rows, :], w_ref[0, :, : 4 * part])
        if chained:
            f += jnp.where(fresh, f_in[...].astype(F32), f_acc[rows, :])
            du += jnp.where(fresh, du_in[...].astype(F32), du_acc[rows, :])
        else:
            f += jnp.where(fresh, 0.0, f_acc[rows, :])
            du += jnp.where(fresh, 0.0, du_acc[rows, :])
        f_acc[rows, :] = f
        du_acc[rows, :] = du
        f_ref[...] = f.astype(BF16)
        du_ref[...] = du.astype(BF16)

    for tile in range(3):

        @pl.when(step == blocks + tile)
        def _():
            if tile < 2:
                out = dot(ut_ref[...], dab[:, 2 * tile * part : (2 * tile + 2) * part])
            else:
                out = dot(gt_ref[...], wh[...])
            dw_ref[0] = out.astype(BF16)


def experts(first_pair, u, g, ut, gt, weights, gates, carried=None):
    pairs, _, cols = weights.shape
    part = cols // 6
    blocks = GROUP // ROWS
    chained = carried is not None
    row = lambda width: pl.BlockSpec((ROWS, width), lambda p, s: (jnp.minimum(s, blocks - 1), 0))
    begin = lambda width: pl.BlockSpec(
        (ROWS, width), lambda p, s: (jnp.where(p == 0, jnp.minimum(s, blocks - 1), blocks - 1), 0)
    )
    finish = lambda width: pl.BlockSpec(
        (ROWS, width), lambda p, s: (jnp.where(p == pairs - 1, jnp.minimum(s, blocks - 1), 0), 0)
    )
    in_specs = [
        row(WIDTH),
        row(WIDTH),
        once((WIDTH, GROUP)),
        once((WIDTH, GROUP)),
        pl.BlockSpec((1, WIDTH, cols), lambda p, s: (p, 0, 0)),
        row(LANES),
    ]
    operands = [u, g, ut, gt, weights, gates]
    if chained:
        in_specs += [begin(WIDTH), begin(WIDTH), begin(LANES)]
        operands += list(carried)
    return pl.pallas_call(
        functools.partial(experts_kernel, first_pair, chained),
        name="experts",
        grid=(pairs, blocks + 3),
        out_shape=(
            jax.ShapeDtypeStruct(weights.shape, BF16),
            jax.ShapeDtypeStruct((GROUP, WIDTH), BF16),
            jax.ShapeDtypeStruct((GROUP, WIDTH), BF16),
            jax.ShapeDtypeStruct((GROUP, LANES), F32),
        ),
        in_specs=in_specs,
        out_specs=(
            pl.BlockSpec((1, WIDTH, 2 * part), lambda p, s: (p, 0, jnp.maximum(s - blocks, 0))),
            finish(WIDTH),
            finish(WIDTH),
            finish(LANES),
        ),
        scratch_shapes=[
            pltpu.VMEM((GROUP, WIDTH), F32),
            pltpu.VMEM((GROUP, WIDTH), F32),
            pltpu.VMEM((GROUP, LANES), F32),
            pltpu.VMEM((GROUP, 4 * part), BF16),
            pltpu.VMEM((GROUP, 2 * part), BF16),
        ],
        compiler_params=params(),
    )(*operands)


def gates_back_kernel(mine_ref, other_ref, gate_ref, keep_ref, ut_ref, dz_ref, router_ref):
    dg = (mine_ref[...] + other_ref[...]) * keep_ref[...]
    gate = gate_ref[...]
    dz = (gate * (dg - jnp.sum(gate * dg, axis=1, keepdims=True))).astype(BF16)
    dz_ref[...] = dz
    router_ref[...] = dot(ut_ref[...], dz)


def gates_back(mine, other, gate, keep, ut):
    return pl.pallas_call(
        gates_back_kernel,
        name="gates_back",
        out_shape=(
            jax.ShapeDtypeStruct((GROUP, LANES), BF16),
            jax.ShapeDtypeStruct((WIDTH, LANES), F32),
        ),
        compiler_params=params(),
    )(mine, other, gate, keep, ut)


def middle_kernel(h_ref, mine_ref, other_ref, dz_ref, r_ref, g_ref, gain_ref,
                  dh_ref, low_ref, lowt_ref, gain_grad_ref):
    h = h_ref[...]
    du = mine_ref[...].astype(F32) + other_ref[...].astype(F32) + dot_nt(dz_ref[...], r_ref[...])
    scale = lax.rsqrt(jnp.mean(h * h, axis=1, keepdims=True) + EPSILON)
    gain = gain_ref[...]
    inner = jnp.mean(du * gain * h, axis=1, keepdims=True)
    dh = g_ref[...].astype(F32) + scale * gain * du - h * (scale * scale * scale) * inner
    dh_ref[...] = dh
    low = dh.astype(BF16)
    low_ref[...] = low
    lowt_ref[...] = low.T
    part = jnp.sum(du * h * scale, axis=0, keepdims=True)
    first = pl.program_id(0) == 0
    gain_grad_ref[...] = jnp.where(first, 0.0, gain_grad_ref[...]) + part


def middle_back(h, mine, other, dz, router, g, gain):
    rows = lambda width: pl.BlockSpec((ROWS, width), lambda i: (i, 0))
    return pl.pallas_call(
        middle_kernel,
        name="middle_back",
        grid=(GROUP // ROWS,),
        out_shape=(
            jax.ShapeDtypeStruct((GROUP, WIDTH), F32),
            jax.ShapeDtypeStruct((GROUP, WIDTH), BF16),
            jax.ShapeDtypeStruct((WIDTH, GROUP), BF16),
            jax.ShapeDtypeStruct((1, WIDTH), F32),
        ),
        in_specs=[
            rows(WIDTH),
            rows(WIDTH),
            rows(WIDTH),
            rows(LANES),
            whole((WIDTH, LANES)),
            rows(WIDTH),
            whole((1, WIDTH)),
        ],
        out_specs=(
            rows(WIDTH),
            rows(WIDTH),
            pl.BlockSpec((WIDTH, ROWS), lambda i: (0, i)),
            whole((1, WIDTH)),
        ),
        compiler_params=params(),
    )(h, mine, other, dz, router, g, gain)


def weights_back_kernel(xnt_ref, lowt_ref, dqkv_ref, o_ref, out_ref):
    width = dqkv_ref.shape[1]
    out_ref[:, :width] = dot(xnt_ref[...], dqkv_ref[...]).astype(BF16)
    out_ref[:, width:] = dot(lowt_ref[...], o_ref[...]).astype(BF16)


def weights_back(xnt, lowt, dqkv, o):
    cols = dqkv.shape[1] + o.shape[1]
    rows = lambda width: pl.BlockSpec((ROWS, width), lambda i: (i, 0))
    return pl.pallas_call(
        weights_back_kernel,
        name="weights_back",
        grid=(WIDTH // ROWS,),
        out_shape=jax.ShapeDtypeStruct((WIDTH, cols), BF16),
        in_specs=[rows(GROUP), rows(GROUP), whole(dqkv.shape), whole(o.shape)],
        out_specs=rows(cols),
        compiler_params=params(),
    )(xnt, lowt, dqkv, o)


def input_kernel(first_ref, d_ref, w_ref, out_ref):
    out_ref[...] = dot_nt(d_ref[...], w_ref[:, : d_ref.shape[1]]).astype(out_ref.dtype)


def input_terms(first_block, dqkv, weights, dtype):
    half = GROUP // 2
    return pl.pallas_call(
        input_kernel,
        name="input_terms",
        grid_spec=pltpu.PrefetchScalarGridSpec(
            num_scalar_prefetch=1,
            grid=(half // ROWS,),
            in_specs=[
                pl.BlockSpec((ROWS, dqkv.shape[1]), lambda i, first: (i + first[0], 0)),
                pl.BlockSpec(weights.shape, lambda i, first: (0, 0)),
            ],
            out_specs=pl.BlockSpec((ROWS, WIDTH), lambda i, first: (i, 0)),
        ),
        out_shape=jax.ShapeDtypeStruct((half, WIDTH), dtype),
        compiler_params=params(),
    )(first_block, dqkv, weights)


def last_kernel(first_ref, d_ref, w_ref, other_ref, x_ref, gain_ref, dh_ref, out_ref, gain_grad_ref):
    x = x_ref[...].astype(F32)
    dxn = dot_nt(d_ref[...], w_ref[:, : d_ref.shape[1]]) + other_ref[...].astype(F32)
    scale = lax.rsqrt(jnp.mean(x * x, axis=1, keepdims=True) + EPSILON)
    gain = gain_ref[...]
    inner = jnp.mean(dxn * gain * x, axis=1, keepdims=True)
    out_ref[...] = dh_ref[...] + scale * gain * dxn - x * (scale * scale * scale) * inner
    part = jnp.sum(dxn * x * scale, axis=0, keepdims=True)
    first = pl.program_id(0) == 0
    gain_grad_ref[...] = jnp.where(first, 0.0, gain_grad_ref[...]) + part


def last(first_block, dqkv, weights, other, x, gain, dh):
    half = GROUP // 2
    local = lambda width: pl.BlockSpec((ROWS, width), lambda i, first: (i, 0))
    shifted = lambda width: pl.BlockSpec((ROWS, width), lambda i, first: (i + first[0], 0))
    return pl.pallas_call(
        last_kernel,
        name="last",
        grid_spec=pltpu.PrefetchScalarGridSpec(
            num_scalar_prefetch=1,
            grid=(half // ROWS,),
            in_specs=[
                shifted(dqkv.shape[1]),
                pl.BlockSpec(weights.shape, lambda i, first: (0, 0)),
                local(WIDTH),
                local(WIDTH),
                pl.BlockSpec((1, WIDTH), lambda i, first: (0, 0)),
                shifted(WIDTH),
            ],
            out_specs=(local(WIDTH), pl.BlockSpec((1, WIDTH), lambda i, first: (0, 0))),
        ),
        out_shape=(
            jax.ShapeDtypeStruct((half, WIDTH), F32),
            jax.ShapeDtypeStruct((1, WIDTH), F32),
        ),
        compiler_params=params(),
    )(first_block, dqkv, weights, other, x, gain, dh)


def shards(
    tokens,
    attn_gain,
    ffn_gain,
    router,
    w_query,
    key_matrix,
    value_matrix,
    w_out_t,
    w_gate,
    w_up,
    w_down_t,
    lengths,
    routes,
    priority,
    cotangent,
):
    me = lax.axis_index("tensor")
    half = tokens.shape[0]
    depth = attn_gain.shape[0]
    q_width = w_query.shape[1]
    part = w_gate.shape[2]

    def swap(v):
        return lax.ppermute(v, "tensor", [(0, 1), (1, 0)])

    def in_order(mine, other):
        return jnp.concatenate(
            [jnp.where(me == 0, mine, other), jnp.where(me == 0, other, mine)], axis=0
        )

    small = jnp.concatenate(
        [router, attn_gain[:, None], ffn_gain[:, None], jnp.zeros((depth, LANES - EXPERTS - 2), BF16)],
        axis=1,
    )
    front = jnp.concatenate([w_query, key_matrix, value_matrix, small], axis=1)
    front_full = lax.all_gather(front, "dp", axis=0, tiled=True)
    out_pair = jnp.concatenate([w_out_t, swap(w_out_t)], axis=1)
    out_full = lax.all_gather(out_pair, "dp", axis=0, tiled=True)
    gate_pair, up_pair, down_pair = (
        w.reshape(EXPERTS // 2, 2, depth, part) for w in (w_gate, w_up, w_down_t)
    )
    packed = jnp.concatenate(
        [gate_pair[:, 0], up_pair[:, 0], gate_pair[:, 1], up_pair[:, 1], down_pair[:, 0], down_pair[:, 1]],
        axis=2,
    )
    pairs = EXPERTS // 4
    experts_a = lax.all_gather(packed[:pairs], "dp", axis=1, tiled=True)
    experts_b = lax.all_gather(packed[pairs:], "dp", axis=1, tiled=True)

    x = in_order(tokens, swap(tokens))
    valid = (jnp.arange(GROUP, dtype=jnp.int32) < lengths[0]).astype(F32)[:, None]
    g = (in_order(cotangent, swap(cotangent)).astype(F32) * valid).astype(BF16)
    gt = g.T
    member_t, keep_t = route(lengths, routes, priority)
    wide = lambda v: jnp.pad(v.T, ((0, 0), (0, LANES - EXPERTS)))
    member, keep = wide(member_t), wide(keep_t)

    frequency = ROPE_BASE ** (-jnp.arange(HEAD // 2, dtype=F32) / (HEAD // 2))
    angles = jnp.arange(GROUP, dtype=F32)[:, None] * frequency[None, :]
    cos_half, sin_half = jnp.cos(angles), jnp.sin(angles)
    cos = jnp.concatenate([cos_half, cos_half], axis=1)
    sin = jnp.concatenate([-sin_half, sin_half], axis=1)

    tail = front_full[:, q_width + 2 * HEAD :]
    gain_one = tail[:, EXPERTS].astype(F32)[None, :]
    gain_two = tail[:, EXPERTS + 1].astype(F32)[None, :]
    router_wide = tail

    xnt, q, k, v = qkv(x, gain_one, front_full, cos, sin, q_width)
    mine, others, lses = [], [], []
    for i in range(2):
        o, lse = attend(i, 2, lengths, q, k, v)
        mine.append(o)
        others.append(swap(o))
        lses.append(lse)
    parts = [
        out_project(i, 2, x, mine[i], others[i], out_full, gain_two, router_wide, member, keep)
        for i in range(2)
    ]
    h, u = (jnp.concatenate([parts[0][i], parts[1][i]], axis=0) for i in range(2))
    ut = jnp.concatenate([parts[0][2], parts[1][2]], axis=1)
    gate, gates = (jnp.concatenate([parts[0][i], parts[1][i]], axis=0) for i in (3, 4))
    o_mine = jnp.concatenate(mine, axis=0)
    lse = jnp.concatenate(lses, axis=1)

    dw_a, f, du, dg = experts(0, u, g, ut, gt, experts_a, gates)
    grads_a = lax.psum_scatter(dw_a, "dp", scatter_dimension=1, tiled=True)
    dw_b, f, du, dg = experts(pairs, u, g, ut, gt, experts_b, gates, (f, du, dg))
    grads_b = lax.psum_scatter(dw_b, "dp", scatter_dimension=1, tiled=True)

    def rows_of(v, index):
        return lax.dynamic_slice_in_dim(v, index * half, half)

    f_other = swap(rows_of(f, 1 - me))
    block_out = (
        rows_of(valid, me) * (rows_of(h, me) + rows_of(f, me).astype(F32) + f_other.astype(F32))
    ).astype(BF16)

    dg_other = wide(swap(dg[:, :EXPERTS].T))
    dz, router_grad = gates_back(dg, dg_other, gate, keep, ut)
    dh, low, lowt, gain_two_grad = middle_back(h, du, swap(du), dz, router_wide, g, gain_two)
    dqkv = attend_back(lengths, low, out_full, q, k, v, lse, cos, sin)
    blocks = half // ROWS
    theirs = input_terms(((1 - me) * blocks)[None], dqkv, front_full, BF16)
    attn_grads = weights_back(xnt, lowt, dqkv, o_mine)
    input_grad, gain_one_grad = last(
        (me * blocks)[None], dqkv, front_full, swap(theirs), tokens, gain_one, dh
    )
    attn_sum = lax.psum_scatter(attn_grads, "dp", scatter_dimension=0, tiled=True)
    gain_one_grad = gain_one_grad + swap(gain_one_grad)
    small_grads = jnp.concatenate(
        [router_grad[:, :EXPERTS], gain_one_grad.T, gain_two_grad.T], axis=1
    )
    small_sum = lax.psum_scatter(small_grads, "dp", scatter_dimension=0, tiled=True)

    grads = jnp.concatenate([grads_a, grads_b], axis=0).astype(F32)
    split = [grads[:, :, i * part : (i + 1) * part] for i in range(6)]
    both = lambda a, b: jnp.stack([split[a], split[b]], axis=1).reshape(EXPERTS, depth, part)
    attn_sum = attn_sum.astype(F32)
    return (
        block_out,
        input_grad,
        small_sum[:, EXPERTS],
        small_sum[:, EXPERTS + 1],
        small_sum[:, :EXPERTS],
        attn_sum[:, :q_width],
        attn_sum[:, q_width : q_width + HEAD],
        attn_sum[:, q_width + HEAD : q_width + 2 * HEAD],
        attn_sum[:, q_width + 2 * HEAD :],
        both(0, 2),
        both(1, 3),
        both(4, 5),
    )


def solution(mesh):
    return jax.shard_map(
        shards,
        mesh=mesh,
        in_specs=(
            P(("dp", "tensor"), None),
            P("dp"),
            P("dp"),
            P("dp", None),
            P("dp", "tensor"),
            P("dp", "tensor"),
            P("dp", "tensor"),
            P("dp", "tensor"),
            P(None, "dp", "tensor"),
            P(None, "dp", "tensor"),
            P(None, "dp", "tensor"),
            P("dp"),
            P("dp", None),
            P("dp", None),
            P(("dp", "tensor"), None),
        ),
        out_specs=(
            P(("dp", "tensor"), None),
            P(("dp", "tensor"), None),
            P("dp"),
            P("dp"),
            P("dp", None),
            P("dp", "tensor"),
            P("dp", "tensor"),
            P("dp", "tensor"),
            P("dp", "tensor"),
            P(None, "dp", "tensor"),
            P(None, "dp", "tensor"),
            P(None, "dp", "tensor"),
        ),
        check_vma=False,
    )
```

time: 2080 us -> 1040 us (0.50)
  local copies, waits for them, and re-layouts: 410 us -> 45.5 us
  waiting for transfers between devices: 995 us -> 698 us
  matrix products: 293 us -> 0 us
  Pallas kernels: 0 us -> 231 us
  blocking collectives: 173 us -> 0 us
  other arithmetic: 185 us -> 24.5 us
    reduce_scatter x11 -> x3, waiting for transfers between devices: 848 us -> 374 us  [the longest x1 149 us: shards(): grads_a = lax.psum_scatter(dw_a, 'dp', scatter_dimension=1, tiled=True)]
    gather x19 -> x0, local copies, waits for them, and re-layouts: 320 us -> none  [the longest x2 64.2 us: shards(): expert_in_grad[slot_rows]]
    dot_general x36 -> x0, matrix products: 291 us -> none  [the longest x1 55.7 us: shards(): jnp.einsum('td,tkd->tk', grad_ffn.astype(FLOAT), picked, precision=lax.Pr...]
    pallas_call x0 -> x14, Pallas kernels: none -> 231 us  [the longest x2 120 us: experts(): pl.pallas_call(functools.partial(experts_kernel, first_pair, chained), na...]
    ppermute x0 -> x10, waiting for transfers between devices: none -> 208 us  [swap(): return lax.ppermute(v, 'tensor', [(0, 1), (1, 0)])]
    reduce_sum x11 -> x0, other arithmetic: 137 us -> none  [the longest x1 63.6 us: shards(): jnp.sum(keep_f[:, :, None] * expert_in_grad[slot_rows], axis=1)]
    unnamed x2 -> x0, blocking collectives: 97.5 us -> none
    all_gather x3 -> x0, blocking collectives: 61.8 us -> none  [the longest x1 21.8 us: gather_layer(): lax.all_gather(value_matrix, 'dp', axis=0, tiled=True)]
  transfers between devices with their start and end apart: 21 -> 18, of which waited for: 12 -> 13; matrix products, arithmetic and copies ran while one was open for 24% -> 5% of each run, Pallas kernels for 0% -> 12%
where the time goes in v1:
time: 1040 us; the launch traced here: 1030 us
  waiting for transfers between devices  698 us (67%)
  Pallas kernels  231 us (22%)
  local copies, waits for them, and re-layouts  45.5 us (4%)
  other arithmetic  24.5 us (2%)
  between operations  15.7 us (2%)
  starting transfers between devices  14.4 us (1%)
    ppermute x10, waiting for transfers between devices, swap(): return lax.ppermute(v, 'tensor', [(0, 1), (1, 0)])  208 us
    reduce_scatter x1, waiting for transfers between devices, shards(): grads_a = lax.psum_scatter(dw_a, 'dp', scatter_dimension=1, tiled=True)  149 us
    reduce_scatter x1, waiting for transfers between devices, shards(): grads_b = lax.psum_scatter(dw_b, 'dp', scatter_dimension=1, tiled=True)  146 us
    pallas_call x2, Pallas kernels, experts(): pl.pallas_call(functools.partial(experts_kernel, first_pair, chained), na...  120 us
    reduce_scatter x1, waiting for transfers between devices, shards(): lax.psum_scatter(attn_grads, 'dp', scatter_dimension=0, tiled=True)  79.7 us
    all_gather x1, waiting for transfers between devices, shards(): experts_a = lax.all_gather(packed[:pairs], 'dp', axis=1, tiled=True)  60.9 us
    all_gather x1, waiting for transfers between devices, shards(): experts_b = lax.all_gather(packed[pairs:], 'dp', axis=1, tiled=True)  52.1 us
    pallas_call x1, Pallas kernels, attend_back(): pl.pallas_call(attend_back_kernel, name='attend_back', grid=(1,), out_sha...  22.5 us
  transfers between devices with their start and end apart: 18, of which 13 were waited for; matrix products, arithmetic and copies ran while one was open for 5% of the time, Pallas kernels for 12%

profile of v1, /device:TPU:0, one launch (start us, length us, event | category | flops | bytes accessed | tf_op | source)
XLA Modules:
  0.0 1029.3 jit_solution(16819596824602842265)
XLA Ops:
  9.7 1.7 concatenate.49
  11.5 3.0 collective-permute-start.2
  14.5 4.1 collective-permute-done.2
  18.5 1.6 pad_maximum_fusion.8
  20.6 1.3 fusion.10
  22.7 1.7 collective-permute-start.4
  25.9 2.0 fusion.8
  27.9 1.3 pad_maximum_fusion.5
  29.2 30.9 %collective-permute-done.4 = bf16[512,1536]{1,0:T(8,128)(2,1)} collective-permute-done((bf16[512,1536]{1,0:T(8,128)(2,1)S(1)}, bf16[512,1536]{1,0:T(8,128)(2,1)}, u32[]{:S(2)}, u32[]{:S(2)}) %collective-permute-start.4) | collective-permute-done | bytes 1572896 | tf_op jit(solution)/shard_map/ppermute | solution.py:597
  60.2 31.9 %collective-permute-done = bf16[512,1536]{1,0:T(8,128)(2,1)} collective-permute-done((bf16[512,1536]{1,0:T(8,128)(2,1)S(1)}, bf16[512,1536]{1,0:T(8,128)(2,1)}, u32[]{:S(2)}, u32[]{:S(2)}) %collective-permute-start) | collective-permute-done | bytes 1572896 | tf_op jit(solution)/shard_map/ppermute | solution.py:597
  92.1 4.0 broadcast_select_fusion.1
  96.0 1.9 pad_maximum_fusion.x_ref
  97.9 1.8 convert_reduce_fusion
  100.4 8.5 qkv.1
  108.9 7.4 attend.2
  116.2 1.4 collective-permute-start.1
  117.7 11.5 %attend.3 = (bf16[512,768]{1,0:T(8,128)(2,1)}, f32[8,512]{1,0:T(8,128)}) custom-call(s32[1]{0:T(128)} %copy.108.length_ref, bf16[1024,768]{1,0:T(8,128)(2,1)} %get-tuple-element.48.q_ref, bf16[1024,128]{1,0:T(8,128)(2,1)} %get-tuple-element.49.k_ref, bf16[1024,128]{1,0:T(8,128)(2,1)} %get-tuple-element.50.v_ref), custom_call_target="tpu_custom_call" | custom-call | tf_op jit(solution)/shard_map/attend/pallas_call | solution.py:160
  129.8 2.9 route.1
  133.7 1.0 copy.75
  136.3 2.5 multiply_convert_fusion.refs_1_.g_ref
  138.8 3.3 copy.83.refs_3_
  142.7 1.8 slice.108.r_ref
  144.5 8.8 out_project.2
  153.3 8.8 out_project.3
  162.1 1.1 constant_dynamic-update-slice_fusion.6.refs_5_
  164.3 1.7 copy-done.15
  166.1 1.7 copy-done.2
  168.0 60.9 %all-gather.11.cloned.1.call-done.refs_4_ = bf16[2,1536,2304]{2,1,0:T(8,128)(2,1)} async-done(((bf16[2,96,2304]{2,1,0:T(8,128)(2,1)}), bf16[2,1536,2304]{2,1,0:T(8,128)(2,1)}) %all-gather.11.cloned.1.call-update) | async-done | bytes 14155792 | tf_op jit(solution)/shard_map/all_gather | solution.py:620
  228.8 59.5 %experts.2 = (bf16[2,1536,2304]{2,1,0:T(8,128)(2,1)}, bf16[1024,1536]{1,0:T(8,128)(2,1)}, bf16[1024,1536]{1,0:T(8,128)(2,1)}, f32[1024,128]{1,0:T(8,128)}) custom-call(bf16[1024,1536]{1,0:T(8,128)(2,1)} %copy-done.2, bf16[1024,1536]{1,0:T(8,128)(2,1)} %copy-done, bf16[1536,1024]{1,0:T(8,128)(2,1)} %copy-done.1, bf16[1536,1024]{1,0:T(8,128)(2,1)} %copy.83.refs_3_, ...), custom_call_target="tpu_custom_call" | custom-call | tf_op jit(solution)/shard_map/experts/pallas_call | solution.py:394
  288.3 52.1 %all-gather.9.cloned.1.call-done.refs_4_ = bf16[2,1536,2304]{2,1,0:T(8,128)(2,1)} async-done(((bf16[2,96,2304]{2,1,0:T(8,128)(2,1)}), bf16[2,1536,2304]{2,1,0:T(8,128)(2,1)}) %all-gather.9.cloned.1.call-update) | async-done | bytes 14155792 | tf_op jit(solution)/shard_map/all_gather | solution.py:621
  340.4 60.7 %experts.3 = (bf16[2,1536,2304]{2,1,0:T(8,128)(2,1)}, bf16[1024,1536]{1,0:T(8,128)(2,1)}, bf16[1024,1536]{1,0:T(8,128)(2,1)}, f32[1024,128]{1,0:T(8,128)}) custom-call(bf16[1024,1536]{1,0:T(8,128)(2,1)} %copy-done.2, bf16[1024,1536]{1,0:T(8,128)(2,1)} %copy-done, bf16[1536,1024]{1,0:T(8,128)(2,1)} %copy-done.1, bf16[1536,1024]{1,0:T(8,128)(2,1)} %copy.83.refs_3_, ...), custom_call_target="tpu_custom_call" | custom-call | tf_op jit(solution)/shard_map/experts/pallas_call | solution.py:394
  401.1 1.5 collective-permute-start.6
  403.3 3.9 constant_dynamic-update-slice_fusion.1
  407.2 2.0 constant_dynamic-update-slice_fusion.h_ref
  410.6 72.3 %collective-permute-done.7 = f32[8,1024]{0,1:T(8,128)S(1)} collective-permute-done((f32[8,1024]{0,1:T(8,128)S(1)}, f32[8,1024]{0,1:T(8,128)S(1)}, u32[]{:S(2)}, u32[]{:S(2)}) %collective-permute-start.7) | collective-permute-done | bytes 32800 | tf_op jit(solution)/shard_map/ppermute | solution.py:597
  483.7 4.5 gates_back.1
  488.3 1.7 copy-done.5
  489.9 12.4 %middle_back.1 = (f32[1024,1536]{1,0:T(8,128)}, bf16[1024,1536]{1,0:T(8,128)(2,1)}, bf16[1536,1024]{1,0:T(8,128)(2,1)}, f32[1,1536]{1,0:T(1,128)}) custom-call(f32[1024,1536]{1,0:T(8,128)} %constant_dynamic-update-slice_fusion.h_ref, bf16[1024,1536]{1,0:T(8,128)(2,1)} %get-tuple-element.67.mine_ref, bf16[1024,1536]{1,0:T(8,128)(2,1)} %copy-done.5, ...), custom_call_target="tpu_custom_call" | custom-call | tf_op jit(solution)/shard_map/middle_back/pallas_call | solution.py:461
  502.4 22.5 %attend_back.1.d_ref.dqkv_ref = bf16[1024,1024]{1,0:T(8,128)(2,1)} custom-call(s32[1]{0:T(128)} %copy.108.length_ref, bf16[1024,1536]{1,0:T(8,128)(2,1)} %get-tuple-element.72.g_ref, bf16[1536,1536]{1,0:T(8,128)(2,1)} %all-gather.7.cloned.1.call-done.wo_ref, bf16[1024,768]{1,0:T(8,128)(2,1)} %get-tuple-element.48.q_ref, ...), custom_call_target="tpu_custom_call" | custom-call | tf_op jit(solution)/shard_map/attend_back/pallas_call | solution.py:224
  524.9 5.1 input_terms.1
  530.0 1.5 collective-permute-start.8
  531.4 34.5 %collective-permute-done.8.other_ref = bf16[512,1536]{1,0:T(8,128)(2,1)S(1)} collective-permute-done((bf16[512,1536]{1,0:T(8,128)(2,1)}, bf16[512,1536]{1,0:T(8,128)(2,1)S(1)}, u32[]{:S(2)}, u32[]{:S(2)}) %collective-permute-start.8) | collective-permute-done | bytes 1572896 | tf_op jit(solution)/shard_map/ppermute | solution.py:597
  566.0 1.1 copy-done.16
  567.1 7.6 last.1
  574.7 1.5 collective-permute-start.9
  576.5 2.2 collective-permute-done.9
  579.4 1.2 copy.88
  580.6 1.2 pad_maximum_fusion.1.o_ref
  581.9 11.2 %weights_back.1 = bf16[1536,1792]{1,0:T(8,128)(2,1)} custom-call(bf16[1536,1024]{1,0:T(8,128)(2,1)} %get-tuple-element.80.xnt_ref, bf16[1536,1024]{1,0:T(8,128)(2,1)} %get-tuple-element.81.lowt_ref, bf16[1024,1024]{1,0:T(8,128)(2,1)} %attend_back.1.d_ref.dqkv_ref, bf16[1024,768]{1,0:T(8,128)(2,1)} %pad_maximum_fusion.1.o_ref), custom_call_target="tpu_custom_call" | custom-call | tf_op jit(solution)/shard_map/weights_back/pallas_call | solution.py:499
  594.6 1.2 copy-done.7
  595.8 1.2 constant_dynamic-slice_fusion
  597.0 1.4 collective-permute-start.5
  598.6 32.5 %collective-permute-done.5 = bf16[512,1536]{1,0:T(8,128)(2,1)} collective-permute-done((bf16[512,1536]{1,0:T(8,128)(2,1)}, bf16[512,1536]{1,0:T(8,128)(2,1)}, u32[]{:S(2)}, u32[]{:S(2)}) %collective-permute-start.5) | collective-permute-done | bytes 1572896 | tf_op jit(solution)/shard_map/ppermute | solution.py:597
  631.0 4.1 multiply_convert_fusion.1
  635.4 1.5 copy.98
  639.0 79.7 %reduce-scatter.7.cloned.1.call-done = bf16[96,1792]{1,0:T(8,128)(2,1)} async-done(((bf16[1536,1792]{1,0:T(8,128)(2,1)}), bf16[96,1792]{1,0:T(8,128)(2,1)}) %reduce-scatter.7.cloned.1.call-update) | async-done | bytes 344080 | tf_op jit(solution)/shard_map/reduce_scatter | solution.py:682
  718.8 1.4 fusion.12
  720.2 1.8 fusion.11
  722.0 145.6 %reduce-scatter.11.cloned.1.call-done = bf16[2,96,2304]{2,1,0:T(8,128)(2,1)} async-done(((bf16[2,1536,2304]{2,1,0:T(8,128)(2,1)}), bf16[2,96,2304]{2,1,0:T(8,128)(2,1)}) %reduce-scatter.11.cloned.1.call-update) | async-done | bytes 884752 | tf_op jit(solution)/shard_map/reduce_scatter | solution.py:662
  867.6 148.9 %reduce-scatter.9.cloned.1.call-done = bf16[2,96,2304]{2,1,0:T(8,128)(2,1)} async-done(((bf16[2,1536,2304]{2,1,0:T(8,128)(2,1)}), bf16[2,96,2304]{2,1,0:T(8,128)(2,1)}) %reduce-scatter.9.cloned.1.call-update) | async-done | bytes 884752 | tf_op jit(solution)/shard_map/reduce_scatter | solution.py:660
  1016.5 1.7 maximum_convert_fusion
  1018.6 1.1 copy.87
  1019.8 1.1 copy.86
  1021.0 1.1 copy.85
  (111 shorter events, 18.9 us)
Async XLA Ops:
  7.2 13.1 %copy-start.18 = (bf16[8,96,384]{2,1,0:T(8,128)(2,1)S(1)}, bf16[8,96,384]{2,1,0:T(8,128)(2,1)}, u32[]{:S(2)}) copy-start(bf16[8,96,384]{2,1,0:T(8,128)(2,1)} %param.23) | copy-start | bytes 1769476
  7.2 13.1 %copy-start.19 = (bf16[8,96,384]{2,1,0:T(8,128)(2,1)S(1)}, bf16[8,96,384]{2,1,0:T(8,128)(2,1)}, u32[]{:S(2)}) copy-start(bf16[8,96,384]{2,1,0:T(8,128)(2,1)} %param.24) | copy-start | bytes 1769476
  7.2 90.7 %all-gather.5.cloned.1.call-start = ((), (), s32[]{:S(2)}) async-start(), calls=%async_computation.4 | async-start | bytes 3760128 | tf_op jit(solution)/shard_map/all_gather | solution.py:609
  11.4 9.1 copy-start.20
  11.4 133.1 %all-gather.7.cloned.1.call-start = ((), (), s32[]{:S(2)}) async-start(), calls=%async_computation.5 | async-start | bytes 5013504 | tf_op jit(solution)/shard_map/all_gather | solution.py:611
  11.5 7.1 collective-permute-start.2
  20.2 208.6 %all-gather.11.cloned.1.call-start = ((), (), s32[]{:S(2)}) async-start(), calls=%async_computation.7 | async-start | bytes 15040512 | tf_op jit(solution)/shard_map/all_gather | solution.py:620
  20.6 2.1 copy-start.11
  21.9 2.5 copy-start.3
  22.0 318.4 %all-gather.9.cloned.1.call-start = ((), (), s32[]{:S(2)}) async-start(), calls=%async_computation.6 | async-start | bytes 15040512 | tf_op jit(solution)/shard_map/all_gather | solution.py:621
  22.5 612.9 %reduce-scatter.13.cloned.1.call-start = ((), (), s32[]{:S(2)}) async-start(), calls=%async_computation.11 | async-start | bytes 835584
  22.7 37.5 %collective-permute-start.4 = (bf16[512,1536]{1,0:T(8,128)(2,1)S(1)}, bf16[512,1536]{1,0:T(8,128)(2,1)}, u32[]{:S(2)}, u32[]{:S(2)}) collective-permute-start(bf16[512,1536]{1,0:T(8,128)(2,1)S(1)} %copy-done.11), channel_id=1, source_target_pairs={{0,1},{1,0},{2,3},{3,2},{4,5},{5,4},{6,7},{7,6},{8,9},{9,8},{10,11... | collective-permute-start | bytes 4718600 | tf_op jit(solution)/shard_map/ppermute | solution.py:597
  24.4 67.6 %collective-permute-start = (bf16[512,1536]{1,0:T(8,128)(2,1)S(1)}, bf16[512,1536]{1,0:T(8,128)(2,1)}, u32[]{:S(2)}, u32[]{:S(2)}) collective-permute-start(bf16[512,1536]{1,0:T(8,128)(2,1)S(1)} %copy-done.3), channel_id=1, source_target_pairs={{0,1},{1,0},{2,3},{3,2},{4,5},{5,4},{6,7},{7,6},{8,9},{9,8},{10,11... | collective-permute-start | bytes 4718600 | tf_op jit(solution)/shard_map/ppermute | solution.py:597
  116.2 28.2 %collective-permute-start.1 = (bf16[512,768]{1,0:T(8,128)(2,1)}, bf16[512,768]{1,0:T(8,128)(2,1)}, u32[]{:S(2)}, u32[]{:S(2)}) collective-permute-start(bf16[512,768]{1,0:T(8,128)(2,1)} %get-tuple-element.51.oa_ref), channel_id=1, source_target_pairs={{0,1},{1,0},{2,3},{3,2},{4,5},{5,4},{6,7},{7,6},{8,9},{9,8},{10,11... | collective-permute-start | bytes 2359304 | tf_op jit(solution)/shard_map/ppermute | solution.py:597
  129.2 24.1 %collective-permute-start.3 = (bf16[512,768]{1,0:T(8,128)(2,1)}, bf16[512,768]{1,0:T(8,128)(2,1)}, u32[]{:S(2)}, u32[]{:S(2)}) collective-permute-start(bf16[512,768]{1,0:T(8,128)(2,1)} %get-tuple-element.55.oa_ref), channel_id=1, source_target_pairs={{0,1},{1,0},{2,3},{3,2},{4,5},{5,4},{6,7},{7,6},{8,9},{9,8},{10,11... | collective-permute-start | bytes 2359304 | tf_op jit(solution)/shard_map/ppermute | solution.py:597
  138.8 3.3 copy-start
  153.3 8.8 copy-start.21
  153.3 10.7 %copy-start.13 = (bf16[512,1536]{1,0:T(8,128)(2,1)S(1)}, bf16[512,1536]{1,0:T(8,128)(2,1)}, u32[]{:S(2)}) copy-start(bf16[512,1536]{1,0:T(8,128)(2,1)} %get-tuple-element.57) | copy-start | bytes 4718596
  162.1 2.0 copy-start.12
  163.2 0.8 copy-start.4
  164.1 1.9 copy-start.15
  164.3 3.4 copy-start.14
  166.1 1.7 copy-start.2
  168.0 60.9 %copy-start.1 = (bf16[1536,1024]{1,0:T(8,128)(2,1)}, bf16[1536,1024]{1,0:T(8,128)(2,1)S(1)}, u32[]{:S(2)}) copy-start(bf16[1536,1024]{1,0:T(8,128)(2,1)S(1)} %constant_dynamic-update-slice_fusion.4.refs_2_.ut_ref) | copy-start | bytes 9437188
  340.4 62.2 %copy-start.24 = (f32[8,512]{1,0:T(8,128)S(1)}, f32[8,512]{1,0:T(8,128)}, u32[]{:S(2)}) copy-start(f32[8,512]{1,0:T(8,128)} %get-tuple-element.73) | copy-start | bytes 49156
  340.4 62.2 %copy-start.25 = (f32[8,512]{1,0:T(8,128)S(1)}, f32[8,512]{1,0:T(8,128)}, u32[]{:S(2)}) copy-start(f32[8,512]{1,0:T(8,128)} %get-tuple-element.74) | copy-start | bytes 49156
  401.1 87.1 %collective-permute-start.6 = (bf16[1024,1536]{1,0:T(8,128)(2,1)}, bf16[1024,1536]{1,0:T(8,128)(2,1)S(1)}, u32[]{:S(2)}, u32[]{:S(2)}) collective-permute-start(bf16[1024,1536]{1,0:T(8,128)(2,1)} %get-tuple-element.67.mine_ref), channel_id=1, source_target_pairs={{0,1},{1,0},{2,3},{3,2},{4,5},{5,4},{6,7},{7,6},{8,9},{9,8},{10,11... | collective-permute-start | bytes 9437192 | tf_op jit(solution)/shard_map/ppermute | solution.py:597
  403.3 3.9 copy-start.6
  407.2 2.0 copy-start.10
  407.2 2.6 copy-start.22
  407.2 2.6 copy-start.23
  409.2 73.7 %collective-permute-start.7 = (f32[8,1024]{0,1:T(8,128)S(1)}, f32[8,1024]{0,1:T(8,128)S(1)}, u32[]{:S(2)}, u32[]{:S(2)}) collective-permute-start(f32[8,1024]{0,1:T(8,128)S(1)} %slice_bitcast_fusion.6), channel_id=1, source_target_pairs={{0,1},{1,0},{2,3},{3,2},{4,5},{5,4},{6,7},{7,6},{8,9},{9,8},{10,11... | collective-permute-start | bytes 98312 | tf_op jit(solution)/shard_map/ppermute | solution.py:597
  488.3 1.7 copy-start.5
  530.0 36.0 %collective-permute-start.8 = (bf16[512,1536]{1,0:T(8,128)(2,1)}, bf16[512,1536]{1,0:T(8,128)(2,1)S(1)}, u32[]{:S(2)}, u32[]{:S(2)}) collective-permute-start(bf16[512,1536]{1,0:T(8,128)(2,1)} %input_terms.1), channel_id=1, source_target_pairs={{0,1},{1,0},{2,3},{3,2},{4,5},{5,4},{6,7},{7,6},{8,9},{9,8},{10,11... | collective-permute-start | bytes 4718600 | tf_op jit(solution)/shard_map/ppermute | solution.py:597
  566.0 1.1 copy-start.16
  567.1 9.1 copy-start.17
  567.1 12.2 %copy-start.26 = (f32[1,1536]{1,0:T(1,128)S(1)}, f32[1,1536]{1,0:T(1,128)}, u32[]{:S(2)}) copy-start(f32[1,1536]{1,0:T(1,128)} %get-tuple-element.79) | copy-start | bytes 18436
  574.7 5.9 copy-start.8
  574.7 5.9 copy-start.9
  574.7 3.9 collective-permute-start.9
  580.6 138.2 %reduce-scatter.7.cloned.1.call-start = ((), (), s32[]{:S(2)}) async-start(), calls=%async_computation.8 | async-start | bytes 5849088 | tf_op jit(solution)/shard_map/reduce_scatter | solution.py:682
  593.1 274.5 %reduce-scatter.11.cloned.1.call-start = ((), (), s32[]{:S(2)}) async-start(), calls=%async_computation.10 | async-start | bytes 15040512 | tf_op jit(solution)/shard_map/reduce_scatter | solution.py:662
  593.8 422.6 %reduce-scatter.9.cloned.1.call-start = ((), (), s32[]{:S(2)}) async-start(), calls=%async_computation.9 | async-start | bytes 15040512 | tf_op jit(solution)/shard_map/reduce_scatter | solution.py:660
  593.9 1.9 copy-start.7
  597.0 34.0 %collective-permute-start.5 = (bf16[512,1536]{1,0:T(8,128)(2,1)}, bf16[512,1536]{1,0:T(8,128)(2,1)}, u32[]{:S(2)}, u32[]{:S(2)}) collective-permute-start(bf16[512,1536]{1,0:T(8,128)(2,1)} %constant_dynamic-slice_fusion), channel_id=1, source_target_pairs={{0,1},{1,0},{2,3},{3,2},{4,5},{5,4},{6,7},{7,6},{8,9},{9,8},{10,11... | collective-permute-start | bytes 4718600 | tf_op jit(solution)/shard_map/ppermute | solution.py:597
Sparse Core Ops, SparseCore 0:
  11.5 49.8 all-gather.4
  64.3 52.3 all-gather.6
  119.6 109.1 all-gather.10
  231.5 108.8 all-gather.8
  580.7 54.7 reduce-scatter.12
  639.7 79.0 reduce-scatter.6
  722.9 144.6 reduce-scatter.10
  871.8 144.6 reduce-scatter.8
